TPU v7x, 256 devices: a whole 4x4x8 slice. The times are simulated.
256 devices in a mesh: seq: 8 (over z), nbr: 32 (over y, x, core).
Axes of the slice: x: 4, y: 4, z: 8, core: 2. Of those that a mesh axis runs over, the one named last changes fastest.
Arguments:
- queries: bfloat16 [32768, 2048], P(('seq', 'nbr')), may hold values from -360 to 360
- d_context: bfloat16 [32768, 2048], P(('seq', 'nbr')), may hold values from -6 to 6
- database: bfloat16 [1024, 128, 1024], P(('seq', 'nbr')), may hold values from -6 to 6
- neighbour_source: int32 [512, 2], P(('seq', 'nbr')), may hold values from 0 to 7, all different within a row; in each aligned block of 2 rows (0 to 1, 2 to 3, ...) at most 2 rows name the same one
- neighbour_slot: int32 [512, 2], P(('seq', 'nbr')), may hold values from 0 to 3
- enc_gain: float32 [1024], replicated, may hold values from 0.1 to 1.9
- kv_weight: bfloat16 [1024, 4096], P('nbr'), may hold values from -0.1875 to 0.1875
Outputs:
- context: bfloat16 [32768, 2048], P(('seq', 'nbr'))
- d_queries: bfloat16 [32768, 2048], P(('seq', 'nbr'))
- d_kv_weight: float32 [1024, 4096], P('nbr')
- d_database: float32 [1024, 128, 1024], P(('seq', 'nbr'))
Inputs may be any that keep to these rules, and one draw needn't show every extreme that they name: `neighbour_source`: A span's 2 neighbours lie on different devices; among the neighbours of one device's spans at most 2 lie on any one device, and exactly 2 on one device in some or all devices.
All inputs are finite; a program needn't handle non-finite values.
Results may differ from a plain program's by a relative error of at most 0.024.
The roundings to bfloat16 on the way count: a program that leaves them out, or rounds other values in their place, can miss the bound.
Values may be sent and summed in bfloat16 or wider, within the bound.
No kernel may reach another device: no remote copies, remote signals or barrier semaphores. Data moves between devices by JAX's collectives and lax.ppermute only.
A program may use at most 128 MiB of HBM per device.

v0:
```python
import jax
import jax.numpy as jnp
from jax import lax
from jax.sharding import PartitionSpec as P

HEAD_DIM = 128
K_NBR = 2


EPSILON = 1e-06


def norm_rows(field_rows, enc_gain):
    mean_square = jnp.mean(field_rows * field_rows, axis=-1, keepdims=True)
    return field_rows * lax.rsqrt(mean_square + EPSILON) * enc_gain


def body(queries, d_context, database, neighbour_source, neighbour_slot, enc_gain, kv_weight):
    seq_count = lax.axis_size("seq")
    span_count = neighbour_source.shape[0]
    request_count = span_count * K_NBR
    capacity = max(2, 4 * span_count // seq_count)
    stored_rows = database.shape[0]
    row_length = database.shape[1]
    feature_width = database.shape[2]
    scale_factor = HEAD_DIM ** (-0.5)
    source_ids = neighbour_source.reshape(request_count)
    slot_ids = neighbour_slot.reshape(request_count)
    position = jnp.arange(request_count, dtype=jnp.int32)
    earlier_same = (source_ids[:, None] == source_ids[None, :]) & (
        position[None, :] < position[:, None]
    )
    bucket_ids = source_ids * capacity + jnp.sum(earlier_same, axis=1)
    bucket_count = seq_count * capacity
    bucket_match = bucket_ids[:, None] == jnp.arange(bucket_count, dtype=jnp.int32)[None, :]
    wanted_slots = jnp.sum(jnp.where(bucket_match, slot_ids[:, None] + 1, 0), axis=0) - 1
    wanted_slots = wanted_slots.reshape(seq_count, capacity)
    requested = lax.all_to_all(wanted_slots, "seq", split_axis=0, concat_axis=0, tiled=True)
    present = requested >= 0
    picked = database[jnp.clip(requested, 0, stored_rows - 1)]
    picked = jnp.where(present[:, :, None, None], picked, jnp.zeros_like(picked))
    arrived = lax.all_to_all(picked, "seq", split_axis=0, concat_axis=0, tiled=True)
    fetched = arrived.reshape(bucket_count, row_length, feature_width)[bucket_ids]
    fetched_wide = fetched.astype(jnp.float32)
    normed = norm_rows(fetched_wide, enc_gain).astype(jnp.bfloat16)
    flat_normed = normed.reshape(request_count * row_length, feature_width)
    weight_full = lax.all_gather(kv_weight, "nbr", axis=0, tiled=True)
    kv_width = weight_full.shape[1] // 2
    head_count = kv_width // HEAD_DIM
    projected = jnp.dot(flat_normed, weight_full, preferred_element_type=jnp.float32).astype(
        jnp.bfloat16
    )
    key_rows = projected[:, :kv_width].reshape(span_count, K_NBR * row_length, head_count, HEAD_DIM)
    value_rows = projected[:, kv_width:].reshape(
        span_count, K_NBR * row_length, head_count, HEAD_DIM
    )
    span_length = queries.shape[0] // span_count
    query_blocks = queries.reshape(span_count, span_length, head_count, HEAD_DIM)
    grad_blocks = d_context.reshape(span_count, span_length, head_count, HEAD_DIM)
    scores = (
        jnp.einsum("cqhd,ckhd->chqk", query_blocks, key_rows, preferred_element_type=jnp.float32)
        * scale_factor
    )
    highest = jnp.max(scores, axis=-1, keepdims=True)
    expanded = jnp.exp(scores - highest)
    probs = expanded / jnp.sum(expanded, axis=-1, keepdims=True)
    probs_half = probs.astype(jnp.bfloat16)
    context = jnp.einsum(
        "chqk,ckhd->cqhd", probs_half, value_rows, preferred_element_type=jnp.float32
    )
    context = context.astype(jnp.bfloat16).reshape(queries.shape)
    d_probs = jnp.einsum(
        "cqhd,ckhd->chqk", grad_blocks, value_rows, preferred_element_type=jnp.float32
    )
    delta = jnp.sum(probs * d_probs, axis=-1, keepdims=True)
    d_scores = (probs * (d_probs - delta) * scale_factor).astype(jnp.bfloat16)
    d_queries = jnp.einsum(
        "chqk,ckhd->cqhd", d_scores, key_rows, preferred_element_type=jnp.float32
    )
    d_queries = d_queries.astype(jnp.bfloat16).reshape(queries.shape)
    d_keys = jnp.einsum(
        "chqk,cqhd->ckhd", d_scores, query_blocks, preferred_element_type=jnp.float32
    ).astype(jnp.bfloat16)
    d_values = jnp.einsum(
        "chqk,cqhd->ckhd", probs_half, grad_blocks, preferred_element_type=jnp.float32
    ).astype(jnp.bfloat16)
    token_count = request_count * row_length
    d_projected = jnp.concatenate(
        [d_keys.reshape(token_count, kv_width), d_values.reshape(token_count, kv_width)], axis=1
    )
    wide_part = lax.psum_scatter(
        lax.dot_general(
            flat_normed, d_projected, (((0,), (0,)), ((), ())), preferred_element_type=jnp.float32
        ).astype(jnp.bfloat16),
        "nbr",
        scatter_dimension=0,
        tiled=True,
    ).astype(jnp.float32)
    d_kv_weight = lax.psum(wide_part, "seq")
    d_normed = lax.dot_general(
        d_projected, weight_full, (((1,), (1,)), ((), ())), preferred_element_type=jnp.float32
    )
    unused, pullback = jax.vjp(lambda field_rows: norm_rows(field_rows, enc_gain), fetched_wide)
    d_fetched = pullback(d_normed.reshape(request_count, row_length, feature_width))[0].astype(
        jnp.bfloat16
    )
    packed = (
        jnp.zeros((bucket_count, row_length, feature_width), jnp.bfloat16)
        .at[bucket_ids]
        .set(d_fetched)
    )
    packed = packed.reshape(seq_count, capacity, row_length, feature_width)
    grads_in, slots_in = (
        lax.all_to_all(packed, "seq", split_axis=0, concat_axis=0, tiled=True),
        lax.all_to_all(wanted_slots, "seq", split_axis=0, concat_axis=0, tiled=True),
    )
    slot_match = (
        jnp.arange(stored_rows, dtype=jnp.int32)[:, None] == slots_in.reshape(bucket_count)[None, :]
    )
    d_database = jnp.einsum(
        "sb,blw->slw",
        slot_match.astype(jnp.bfloat16),
        grads_in.reshape(bucket_count, row_length, feature_width),
        preferred_element_type=jnp.float32,
    )
    return (context, d_queries, d_kv_weight, d_database)


def solution(mesh):
    return jax.shard_map(
        body,
        mesh=mesh,
        in_specs=(
            P(("seq", "nbr"), None),
            P(("seq", "nbr"), None),
            P(("seq", "nbr"), None, None),
            P(("seq", "nbr"), None),
            P(("seq", "nbr"), None),
            P(),
            P("nbr", None),
        ),
        out_specs=(
            P(("seq", "nbr"), None),
            P(("seq", "nbr"), None),
            P("nbr", None),
            P(("seq", "nbr"), None, None),
        ),
        check_vma=False,
    )
```

profile of v0, /device:TPU:2, one launch (start us, length us, event | category | flops | bytes accessed | tf_op | source)
XLA Modules:
  0.0 381.8 jit_solution(1486818155061373319)
XLA Ops:
  9.8 15.9 %all_to_all.17 = s32[8,1,2]{2,1,0:T(1,128)S(1)} all-to-all(s32[8,1,2]{2,1,0:T(1,128)S(1)} %bitcast.146), channel_id=1, replica_groups=mesh['seq'=8,'nbr'=32] {'seq'}, dimensions={0} | all-to-all | bytes 128 | tf_op jit(solution)/shard_map/all_to_all | solution.py:38
  26.1 2.8 gather_fusion
  28.9 4.5 %broadcast_select_fusion = bf16[8,2,128,1024]{3,2,1,0:T(8,128)(2,1)} fusion(bf16[8,2,128,1024]{3,2,1,0:T(8,128)(2,1)} %bitcast.130, pred[8,2]{1,0:T(8,128)(4,1)S(1)} %copy.84), kind=kLoop, calls=%fused_computation.7 | loop fusion | flops 2097152 | bytes 8388624 | tf_op jit(solution)/shard_map/jit(_where)/select_n | solution.py:41
  33.4 4.7 %all-to-all-start.1 = ((bf16[8,2,128,1024]{3,2,1,0:T(8,128)(2,1)}), bf16[8,2,128,1024]{3,2,1,0:T(8,128)(2,1)}, u32[]{:S(2)}, u32[]{:S(2)}) async-start(bf16[8,2,128,1024]{3,2,1,0:T(8,128)(2,1)} %broadcast_select_fusion), calls=%async_computation.1 | async-start | bytes 8388608 | tf_op jit(solution)/shard_map/all_to_all | solution.py:42
  40.1 93.1 %all-to-all-done.1 = bf16[8,2,128,1024]{3,2,1,0:T(8,128)(2,1)} async-done(((bf16[8,2,128,1024]{3,2,1,0:T(8,128)(2,1)}), bf16[8,2,128,1024]{3,2,1,0:T(8,128)(2,1)}, u32[]{:S(2)}, u32[]{:S(2)}) %all-to-all-start.1) | async-done | bytes 4194336 | tf_op jit(solution)/shard_map/all_to_all | solution.py:42
  133.2 2.8 gather_fusion.1
  136.6 8.6 %convolution_convert_fusion.1 = bf16[512,4096]{1,0:T(8,128)(2,1)S(1)} fusion(bf16[512,1024]{1,0:T(8,128)(2,1)S(1)} %fusion.10, bf16[1024,4096]{1,0:T(8,128)(2,1)} %all-gather.2.cloned.1.call-done), kind=kOutput, calls=%fused_computation.6 | convolution fusion | flops 4297064448 | bytes 13631488 | tf_op jit(solution)/shard_map/dot_general | solution.py:50
  153.0 8.0 %convert_bitcast_fusion = bf16[2,256,16,128]{3,1,2,0:T(8,128)(2,1)} fusion(bf16[2,64,16,128]{3,2,1,0:T(8,128)(2,1)} %bitcast.139, f32[2,16,64]{2,1,0:T(8,128)S(1)} %get-tuple-element.28, f32[2,16,256,64]{2,3,1,0:T(8,128)} %copy-done.2), kind=kOutput, calls=%fused_computation.31 | convolution fusion | flops 137890048 | bytes 4726784 | tf_op jit(solution)/shard_map/chqk,cqhd->ckhd/dot_general | solution.py:84
  161.0 17.1 %convert_bitcast_fusion.1 = bf16[2,256,16,128]{3,1,2,0:T(8,128)(2,1)} fusion(f32[2,16,256,64]{2,3,1,0:T(8,128)} %fusion.15, bf16[2,64,16,128]{3,2,1,0:T(8,128)(2,1)} %bitcast.137, f32[2,16,64,256]{3,2,1,0:T(8,128)} %get-tuple-element.29, f32[2,16,64]{2,1,0:T(8,128)S(1)} %get-tuple-element.28), kind=kOutput, calls=%fused_computation.32 | convolution fusion | flops 138938624 | bytes 6823936 | tf_op jit(solution)/shard_map/chqk,cqhd->ckhd/dot_general | solution.py:81
  178.0 3.1 copy.96
  185.5 6.9 %convolution_convert_fusion = bf16[1024,4096]{1,0:T(8,128)(2,1)} fusion(bf16[512,1024]{1,0:T(8,128)(2,1)S(1)} %copy-done.9, bf16[512,4096]{1,0:T(8,128)(2,1)S(1)} %bitcast_dynamic-update-slice_fusion), kind=kOutput, calls=%fused_computation.5 | convolution fusion | flops 4299161600 | bytes 13631488 | tf_op jit(solution)/shard_map/dot_general | solution.py:92
  192.4 8.4 %fusion.11 = (f32[512]{0:T(512)S(1)}, f32[512,1024]{1,0:T(8,128)S(1)}) fusion(bf16[4,128,1024]{2,1,0:T(8,128)(2,1)S(1)} %gather_fusion.1, f32[1024]{0:T(1024)S(1)} %copy-done.13, bf16[512,4096]{1,0:T(8,128)(2,1)} %copy-done.10, bf16[1024,4096]{1,0:T(8,128)(2,1)} %all-gather.2.cloned.1.call-done), kind=kOutput, calls=%fused_computation.30 | convolution fusion | flops 4297063936 | bytes 15734784 | tf_op jit(solution)/shard_map/dot_general | solution.py:100
  202.4 2.5 broadcast_in_dim.30
  204.9 2.8 scatter_fusion
  207.8 8.7 %copy.99 = bf16[8,2,128,1024]{3,1,2,0:T(2,128)(2,1)} copy(bf16[8,2,128,1024]{3,2,1,0:T(8,128)(2,1)} %bitcast.129) | data formatting | bytes 8388608 | tf_op jit(solution)/shard_map/reshape | solution.py:112
  216.4 4.9 %all-to-all-start.2 = ((bf16[8,2,128,1024]{3,1,2,0:T(2,128)(2,1)}), bf16[8,2,128,1024]{3,1,2,0:T(2,128)(2,1)}, u32[]{:S(2)}, u32[]{:S(2)}) async-start(bf16[8,2,128,1024]{3,1,2,0:T(2,128)(2,1)} %copy.99), calls=%async_computation.3 | async-start | bytes 8388608 | tf_op jit(solution)/shard_map/all_to_all | solution.py:114
  222.6 15.8 %fusion.32 = bf16[2,64,16,128]{3,1,2,0:T(8,128)(2,1)S(1)} fusion(bf16[2,256,16,128]{3,2,1,0:T(8,128)(2,1)} %bitcast.134, f32[2,16,256,64]{2,3,1,0:T(8,128)} %fusion.15, f32[2,16,64,256]{3,2,1,0:T(8,128)} %get-tuple-element.29, f32[2,16,64]{2,1,0:T(8,128)S(1)} %get-tuple-element.28), kind=kOutput, calls=%fused_computation.45 | convolution fusion | flops 138152192 | bytes 6823936 | tf_op jit(solution)/shard_map/chqk,ckhd->cqhd/dot_general | solution.py:77
  238.8 6.7 %fusion.29 = bf16[2,64,16,128]{3,1,2,0:T(8,128)(2,1)} fusion(bf16[2,256,16,128]{3,2,1,0:T(8,128)(2,1)S(1)} %bitcast.132, f32[2,16,64]{2,1,0:T(8,128)S(1)} %get-tuple-element.28, f32[2,16,256,64]{2,3,1,0:T(8,128)} %copy-done.2), kind=kOutput, calls=%fused_computation.44 | convolution fusion | flops 137103616 | bytes 4726784 | tf_op jit(solution)/shard_map/chqk,ckhd->cqhd/dot_general | solution.py:68
  248.0 69.9 %all-to-all-done.2 = bf16[8,2,128,1024]{3,1,2,0:T(2,128)(2,1)} async-done(((bf16[8,2,128,1024]{3,1,2,0:T(2,128)(2,1)}), bf16[8,2,128,1024]{3,1,2,0:T(2,128)(2,1)}, u32[]{:S(2)}, u32[]{:S(2)}) %all-to-all-start.2) | async-done | bytes 4194336 | tf_op jit(solution)/shard_map/all_to_all | solution.py:114
  318.0 8.9 %copy.100 = bf16[8,2,128,1024]{3,1,0,2:T(2,128)(2,1)} copy(bf16[8,2,128,1024]{3,1,2,0:T(2,128)(2,1)} %all-to-all-done.2) | data formatting | bytes 8388608 | tf_op jit(solution)/shard_map/all_to_all | solution.py:114
  326.9 7.2 %reshape.184 = bf16[16,128,1024]{2,0,1:T(8,128)(2,1)} reshape(bf16[8,2,128,1024]{3,1,0,2:T(2,128)(2,1)} %copy.100) | data formatting | bytes 8388608 | tf_op jit(solution)/shard_map/reshape | solution.py:123
  334.1 3.0 fusion.46
  337.1 2.5 copy.101
  339.7 34.8 %all-reduce.1 = f32[32,4096]{1,0:T(8,128)} all-reduce(bf16[32,4096]{1,0:T(8,128)(2,1)} %reduce-scatter.2.cloned.1.call-done), channel_id=1, replica_groups=mesh['seq'=8,'nbr'=32] {'seq'}, use_global_device_ids=true, to_apply=%region_7.8 | all-reduce | flops 131072 | bytes 786432 | tf_op jit(solution)/shard_map/psum | solution.py:99
  (77 shorter events, 23.3 us)
Async XLA Ops:
  7.2 19.0 %copy-start = (bf16[4,128,1024]{2,1,0:T(8,128)(2,1)S(1)}, bf16[4,128,1024]{2,1,0:T(8,128)(2,1)}, u32[]{:S(2)}) copy-start(bf16[4,128,1024]{2,1,0:T(8,128)(2,1)} %param.9) | copy-start | bytes 3145732
  7.2 129.5 %all-gather.2.cloned.1.call-start = ((), (), s32[]{:S(2)}) async-start(), calls=%async_computation.4 | async-start | bytes 8650752 | tf_op jit(solution)/shard_map/all_gather | solution.py:47
  33.4 4.8 %copy-start.14 = (s32[2,2]{1,0:T(2,128)S(1)}, s32[2,2]{1,0:T(2,128)}, u32[]{:S(2)}) copy-start(s32[2,2]{1,0:T(2,128)} %param.10) | copy-start | bytes 52
  33.4 4.9 %copy-start.11 = (bf16[128,2048]{1,0:T(8,128)(2,1)S(1)}, bf16[128,2048]{1,0:T(8,128)(2,1)}, u32[]{:S(2)}) copy-start(bf16[128,2048]{1,0:T(8,128)(2,1)} %param.7) | copy-start | bytes 1572868
  33.4 5.8 %copy-start.12 = (bf16[128,2048]{1,0:T(8,128)(2,1)S(1)}, bf16[128,2048]{1,0:T(8,128)(2,1)}, u32[]{:S(2)}) copy-start(bf16[128,2048]{1,0:T(8,128)(2,1)} %param.8) | copy-start | bytes 1572868
  33.4 99.8 %all-to-all-start.1 = ((bf16[8,2,128,1024]{3,2,1,0:T(8,128)(2,1)}), bf16[8,2,128,1024]{3,2,1,0:T(8,128)(2,1)}, u32[]{:S(2)}, u32[]{:S(2)}) async-start(bf16[8,2,128,1024]{3,2,1,0:T(8,128)(2,1)} %broadcast_select_fusion), calls=%async_computation.1 | async-start | bytes 8388608 | tf_op jit(solution)/shard_map/all_to_all | solution.py:42
  38.1 301.6 %reduce-scatter.2.cloned.1.call-start = ((), (), s32[]{:S(2)}) async-start(), calls=%async_computation.5 | async-start | bytes 8650752 | tf_op jit(solution)/shard_map/reduce_scatter | solution.py:91
  39.1 97.1 %copy-start.13 = (f32[1024]{0:T(1024)S(1)}, f32[1024]{0:T(1024)}, u32[]{:S(2)}) copy-start(f32[1024]{0:T(1024)} %param.12) | copy-start | bytes 12292
  136.6 8.7 %copy-start.8 = (bf16[512,1024]{1,0:T(8,128)(2,1)}, bf16[512,1024]{1,0:T(8,128)(2,1)S(1)}, u32[]{:S(2)}) copy-start(bf16[512,1024]{1,0:T(8,128)(2,1)S(1)} %fusion.10) | copy-start | bytes 3145732
  146.5 1.3 copy-start.3
  146.5 1.4 copy-start.5
  148.8 2.0 copy-start.2
  148.8 2.0 copy-start.6
  178.0 3.1 copy-start.7
  183.0 2.5 copy-start.9
  183.5 1.9 copy-start.10
  202.4 2.5 copy-start.4
  216.4 101.5 %all-to-all-start.2 = ((bf16[8,2,128,1024]{3,1,2,0:T(2,128)(2,1)}), bf16[8,2,128,1024]{3,1,2,0:T(2,128)(2,1)}, u32[]{:S(2)}, u32[]{:S(2)}) async-start(bf16[8,2,128,1024]{3,1,2,0:T(2,128)(2,1)} %copy.99), calls=%async_computation.3 | async-start | bytes 8388608 | tf_op jit(solution)/shard_map/all_to_all | solution.py:114
  334.1 40.4 %copy-start.1 = (bf16[4,128,1024]{2,1,0:T(8,128)(2,1)S(1)}, bf16[4,128,1024]{2,1,0:T(8,128)(2,1)}, u32[]{:S(2)}) copy-start(bf16[4,128,1024]{2,1,0:T(8,128)(2,1)} %param.9) | copy-start | bytes 3145732
Sparse Core Ops, SparseCore 0:
  10.6 60.8 all-gather.1
  192.6 96.2 reduce-scatter.1
where the time goes:
time: 386 us; the launch traced here: 382 us
  waiting for transfers between devices  164 us (42%)
  matrix products  77.5 us (20%)
  local copies, waits for them, and re-layouts  55.1 us (14%)
  blocking collectives  50.8 us (13%)
  between operations  14.7 us (4%)
  other arithmetic  10.2 us (3%)
  starting transfers between devices  9.66 us (3%)
    all_to_all x1, waiting for transfers between devices, body(): lax.all_to_all(picked, 'seq', split_axis=0, concat_axis=0, tiled=True)  93.1 us
    all_to_all x1, waiting for transfers between devices, body(): lax.all_to_all(packed, 'seq', split_axis=0, concat_axis=0, tiled=True)  69.9 us
    psum x1, blocking collectives, body(): d_kv_weight = lax.psum(wide_part, 'seq')  34.8 us
    dot_general x1, matrix products, body(): jnp.einsum('chqk,cqhd->ckhd', d_scores, query_blocks, preferred_element_t...  17.1 us
    all_to_all x1, blocking collectives, body(): lax.all_to_all(wanted_slots, 'seq', split_axis=0, concat_axis=0, tiled=True)  15.9 us
    dot_general x1, matrix products, body(): jnp.einsum('chqk,ckhd->cqhd', d_scores, key_rows, preferred_element_type=...  15.8 us
    unnamed x37, local copies, waits for them, and re-layouts  9.54 us
    all_to_all x1, local copies, waits for them, and re-layouts, body(): lax.all_to_all(packed, 'seq', split_axis=0, concat_axis=0, tiled=True)  8.87 us
  transfers between devices with their start and end apart: 4, of which 2 were waited for; matrix products, arithmetic and copies ran while one was open for 23% of the time, Pallas kernels for 0%

commit v1 on v0

v1 whole, which is shorter than its diff:
```python
import functools

import jax
import jax.numpy as jnp
from jax import lax
from jax.experimental import pallas as pl
from jax.experimental.pallas import tpu as pltpu
from jax.sharding import PartitionSpec as P

HEAD_DIM = 128
K_NBR = 2
EPSILON = 1e-06
HEADS_STEP = 2
X_CHIPS = 4
Y_CHIPS = 4
F32 = jnp.float32
BF16 = jnp.bfloat16


def mm(a, b, ca, cb):
    return lax.dot_general(a, b, (((ca,), (cb,)), ((), ())), preferred_element_type=F32)


def pick_kernel(ids_ref, stored_ref, out_ref, *, peers, stored, requests, piece):
    for peer in range(peers):
        for r in range(requests):
            row = ids_ref[peer * requests + r]
            source = lax.div(row, stored)
            start = pl.multiple_of(lax.rem(row, stored) * piece, piece)
            out_ref[peer, pl.ds(r * piece, piece), :] = stored_ref[source, pl.ds(start, piece), :]


def sum_kernel(ids_ref, grads_ref, out_ref, total_ref, *, peers, requests, piece):
    total_ref[...] = jnp.zeros_like(total_ref)
    for peer in range(peers):
        for r in range(requests):
            row = ids_ref[peer * requests + r]
            total_ref[row] += grads_ref[peer, pl.ds(r * piece, piece), :].astype(F32)
    out_ref[...] = total_ref[...].astype(BF16).reshape(out_ref.shape)


def main_kernel(
    core_ref,
    rows_ref,
    gain_ref,
    wk_ref,
    wv_ref,
    q_ref,
    g_ref,
    ctx_ref,
    dq_ref,
    own_k_ref,
    oth_k_ref,
    own_v_ref,
    oth_v_ref,
    dfet_ref,
    normed_ref,
    normed_t_ref,
    dnormed_ref,
    dk_ref,
    dv_ref,
    *,
    spans,
    span_length,
):
    step = pl.program_id(0)
    scale_factor = HEAD_DIM ** (-0.5)
    positions = normed_ref.shape[0] // spans
    width = rows_ref.shape[-1]
    gain = gain_ref[...]

    def wide_rows(c):
        return rows_ref[:, c].astype(F32).reshape(positions, width)

    @pl.when(step == 0)
    def _():
        for c in range(spans):
            x = wide_rows(c)
            r = lax.rsqrt(jnp.mean(x * x, axis=-1, keepdims=True) + EPSILON)
            normed = (x * r * gain).astype(BF16)
            normed_ref[pl.ds(c * positions, positions), :] = normed
            normed_t_ref[:, pl.ds(c * positions, positions)] = normed.T
        dnormed_ref[...] = jnp.zeros_like(dnormed_ref)

    normed = normed_ref[...]
    keys = mm(normed, wk_ref[...], 1, 0).astype(BF16)
    values = mm(normed, wv_ref[...], 1, 0).astype(BF16)
    for c in range(spans):
        for h in range(HEADS_STEP):
            toks = slice(c * span_length, (c + 1) * span_length)
            poss = slice(c * positions, (c + 1) * positions)
            cols = slice(h * HEAD_DIM, (h + 1) * HEAD_DIM)
            q = q_ref[toks, cols]
            g = g_ref[toks, cols]
            k = keys[poss, cols]
            v = values[poss, cols]
            scores = mm(q, k, 1, 1) * scale_factor
            expanded = jnp.exp(scores - jnp.max(scores, axis=-1, keepdims=True))
            probs = expanded / jnp.sum(expanded, axis=-1, keepdims=True)
            probs_half = probs.astype(BF16)
            ctx_ref[toks, cols] = mm(probs_half, v, 1, 0).astype(BF16)
            d_probs = mm(g, v, 1, 1)
            delta = jnp.sum(probs * d_probs, axis=-1, keepdims=True)
            d_scores = (probs * (d_probs - delta) * scale_factor).astype(BF16)
            dq_ref[toks, cols] = mm(d_scores, k, 1, 0).astype(BF16)
            dk_ref[poss, cols] = mm(d_scores, q, 0, 0).astype(BF16)
            dv_ref[poss, cols] = mm(probs_half, g, 0, 0).astype(BF16)
    dk = dk_ref[...]
    dv = dv_ref[...]
    dnormed_ref[...] += mm(dk, wk_ref[...], 1, 1) + mm(dv, wv_ref[...], 1, 1)
    shape = own_k_ref.shape
    for grad, own_ref, oth_ref in ((dk, own_k_ref, oth_k_ref), (dv, own_v_ref, oth_v_ref)):
        term = mm(normed_t_ref[...], grad, 1, 0).astype(BF16)
        term = term.reshape(shape[0], 2, shape[1], shape[2])

        @pl.when(core_ref[0] == 0)
        def _():
            own_ref[...] = term[:, 0]
            oth_ref[...] = term[:, 1]

        @pl.when(core_ref[0] != 0)
        def _():
            own_ref[...] = term[:, 1]
            oth_ref[...] = term[:, 0]

    @pl.when(step == pl.num_programs(0) - 1)
    def _():
        for c in range(spans):
            x = wide_rows(c)
            r = lax.rsqrt(jnp.mean(x * x, axis=-1, keepdims=True) + EPSILON)
            dng = dnormed_ref[pl.ds(c * positions, positions), :] * gain
            inner = jnp.sum(dng * x, axis=-1, keepdims=True)
            dx = r * dng - x * (r * r * r * inner * (1.0 / width))
            dfet_ref[:, c] = dx.astype(BF16).reshape(dfet_ref.shape[0], *dfet_ref.shape[2:])


def ring_sum(blocks, axis, position, plus, minus):
    b = [
        lax.dynamic_index_in_dim(blocks, (position + d) % 4, axis, keepdims=False)
        for d in range(4)
    ]
    half = blocks.shape[-1] // 2
    up = lax.ppermute(b[2][..., :half], "nbr", plus)
    down = lax.ppermute(b[2][..., half:], "nbr", minus)
    first = jnp.concatenate([b[1][..., :half] + up, b[1][..., half:]], axis=-1)
    third = jnp.concatenate([b[3][..., :half], b[3][..., half:] + down], axis=-1)
    from_low = lax.ppermute(first, "nbr", plus)
    from_high = lax.ppermute(third, "nbr", minus)
    total = b[0].astype(F32) + from_low.astype(F32) + from_high.astype(F32)
    return total.astype(BF16)


def swap(array):
    return lax.all_to_all(array, "seq", split_axis=0, concat_axis=0, tiled=True)


def body(queries, d_context, database, neighbour_source, neighbour_slot, enc_gain, kv_weight):
    peers = lax.axis_size("seq")
    spans = neighbour_source.shape[0]
    requests = spans * K_NBR
    stored, row_length, width = database.shape
    piece = row_length // peers
    span_length = queries.shape[0] // spans
    kv_width = kv_weight.shape[1] // 2
    me = lax.axis_index("nbr")
    core = me % 2
    x_at = (me // 2) % X_CHIPS
    y_at = me // (2 * X_CHIPS)
    chips = X_CHIPS * Y_CHIPS
    shard_rows = kv_weight.shape[0]

    weight_full = lax.all_gather(kv_weight, "nbr", axis=0, tiled=True)

    wanted = (neighbour_source * stored + neighbour_slot).reshape(1, 1, requests)
    note = jnp.pad(wanted.astype(BF16), ((0, 0), (0, 7), (0, width - requests)))
    note = jnp.broadcast_to(note, (peers, 8, width))
    pieces = database.reshape(stored, peers, piece, width).transpose(1, 0, 2, 3)
    pieces = pieces.reshape(peers, stored * piece, width)
    held = swap(jnp.concatenate([pieces, note], axis=1))
    ids = held[:, stored * piece, :requests].astype(jnp.int32).reshape(peers * requests)
    ids = jnp.clip(ids, 0, peers * stored - 1)

    smem = pl.BlockSpec(memory_space=pltpu.SMEM)
    vmem = pl.BlockSpec(memory_space=pltpu.VMEM)
    picked = pl.pallas_call(
        functools.partial(pick_kernel, peers=peers, stored=stored, requests=requests, piece=piece),
        out_shape=jax.ShapeDtypeStruct((peers, requests * piece, width), BF16),
        in_specs=[smem, vmem],
        out_specs=vmem,
        compiler_params=pltpu.CompilerParams(vmem_limit_bytes=16 << 20),
        cost_estimate=pl.CostEstimate(flops=0, bytes_accessed=4 << 20, transcendentals=0),
        name="pick",
    )(ids, held)
    rows = swap(picked).reshape(peers, spans, K_NBR * piece, width)

    tokens = requests * row_length
    step_cols = HEADS_STEP * HEAD_DIM
    steps = kv_width // step_cols
    half_shape = jax.ShapeDtypeStruct((chips, shard_rows, kv_width), BF16)
    half_spec = pl.BlockSpec((chips, shard_rows, step_cols), lambda i: (0, 0, i))
    token_spec = pl.BlockSpec((queries.shape[0], step_cols), lambda i: (0, i))
    whole = pl.BlockSpec(rows.shape, lambda i: (0, 0, 0, 0))
    context, d_queries, own_k, oth_k, own_v, oth_v, d_rows = pl.pallas_call(
        functools.partial(main_kernel, spans=spans, span_length=span_length),
        grid=(steps,),
        out_shape=[
            jax.ShapeDtypeStruct(queries.shape, BF16),
            jax.ShapeDtypeStruct(queries.shape, BF16),
            half_shape,
            half_shape,
            half_shape,
            half_shape,
            jax.ShapeDtypeStruct(rows.shape, BF16),
        ],
        in_specs=[
            smem,
            whole,
            pl.BlockSpec((1, width), lambda i: (0, 0)),
            pl.BlockSpec((width, step_cols), lambda i: (0, i)),
            pl.BlockSpec((width, step_cols), lambda i: (0, steps + i)),
            token_spec,
            token_spec,
        ],
        out_specs=[token_spec, token_spec, half_spec, half_spec, half_spec, half_spec, whole],
        scratch_shapes=[
            pltpu.VMEM((tokens, width), BF16),
            pltpu.VMEM((width, tokens), BF16),
            pltpu.VMEM((tokens, width), F32),
            pltpu.VMEM((tokens, step_cols), BF16),
            pltpu.VMEM((tokens, step_cols), BF16),
        ],
        compiler_params=pltpu.CompilerParams(vmem_limit_bytes=48 << 20),
        cost_estimate=pl.CostEstimate(
            flops=14_000_000_000, bytes_accessed=24 << 20, transcendentals=1 << 20
        ),
        name="attend",
    )(core.reshape(1), rows, enc_gain.reshape(1, width), weight_full, weight_full, queries, d_context)

    returned = swap(d_rows.reshape(peers, requests * piece, width))

    pair = [(i, i ^ 1) for i in range(2 * chips)]

    def shifted(dx, dy):
        moves = []
        for y in range(Y_CHIPS):
            for x in range(X_CHIPS):
                for k in range(2):
                    to_chip = ((y + dy) % Y_CHIPS) * X_CHIPS + (x + dx) % X_CHIPS
                    moves.append(((y * X_CHIPS + x) * 2 + k, to_chip * 2 + k))
        return moves

    grid4 = (Y_CHIPS, X_CHIPS, shard_rows, kv_width)
    got_k = lax.ppermute(oth_k, "nbr", pair)
    got_v = lax.ppermute(oth_v, "nbr", pair)
    sum_k = (own_k.astype(F32) + got_k.astype(F32)).astype(BF16).reshape(grid4)
    sum_v = (own_v.astype(F32) + got_v.astype(F32)).astype(BF16).reshape(grid4)
    xp, xm, yp, ym = shifted(1, 0), shifted(-1, 0), shifted(0, 1), shifted(0, -1)
    part_k = ring_sum(sum_k, 1, x_at, xp, xm)
    part_v = ring_sum(sum_v, 0, y_at, yp, ym)
    part_k = ring_sum(part_k, 0, y_at, yp, ym)
    part_v = ring_sum(part_v, 0, x_at, xp, xm)
    part = jnp.concatenate([part_k, part_v], axis=1)
    cut = part.shape[1] // peers
    part = swap(part.reshape(shard_rows, peers, cut).transpose(1, 0, 2))
    part = jnp.sum(part.astype(F32), axis=0)
    part = swap(jnp.broadcast_to(part[None], (peers, shard_rows, cut)))
    d_kv_weight = part.transpose(1, 0, 2).reshape(shard_rows, peers * cut)

    summed = pl.pallas_call(
        functools.partial(sum_kernel, peers=peers, requests=requests, piece=piece),
        out_shape=jax.ShapeDtypeStruct((peers, stored * piece, width), BF16),
        in_specs=[smem, vmem],
        out_specs=vmem,
        scratch_shapes=[pltpu.VMEM((peers * stored, piece, width), F32)],
        compiler_params=pltpu.CompilerParams(vmem_limit_bytes=16 << 20),
        cost_estimate=pl.CostEstimate(flops=0, bytes_accessed=4 << 20, transcendentals=0),
        name="add_rows",
    )(ids, returned)
    final = swap(summed).reshape(peers, stored, piece, width)
    d_database = final.transpose(1, 0, 2, 3).reshape(database.shape).astype(F32)
    return context, d_queries, d_kv_weight, d_database


def solution(mesh):
    return jax.shard_map(
        body,
        mesh=mesh,
        in_specs=(
            P(("seq", "nbr"), None),
            P(("seq", "nbr"), None),
            P(("seq", "nbr"), None, None),
            P(("seq", "nbr"), None),
            P(("seq", "nbr"), None),
            P(),
            P("nbr", None),
        ),
        out_specs=(
            P(("seq", "nbr"), None),
            P(("seq", "nbr"), None),
            P("nbr", None),
            P(("seq", "nbr"), None, None),
        ),
        check_vma=False,
    )
```

time: 386 us -> 245 us (0.63)
  waiting for transfers between devices: 164 us -> 85.4 us
  matrix products: 77.5 us -> 0 us
  local copies, waits for them, and re-layouts: 55.1 us -> 9.07 us
  Pallas kernels: 0 us -> 44.4 us
  starting transfers between devices: 9.66 us -> 43.7 us
  blocking collectives: 50.8 us -> 39.8 us
  other arithmetic: 10.2 us -> 6.19 us
    all_to_all x2 -> x5, waiting for transfers between devices: 163 us -> 70.2 us  [swap(): return lax.all_to_all(array, 'seq', split_axis=0, concat_axis=0, tiled=True)]
    dot_general x10 -> x0, matrix products: 77.5 us -> none  [the longest x1 17.1 us: body(): jnp.einsum('chqk,cqhd->ckhd', d_scores, query_blocks, preferred_element_t...]
    pallas_call x0 -> x3, Pallas kernels: none -> 44.4 us  [the longest x1 40.8 us: body(): pl.pallas_call(functools.partial(main_kernel, spans=spans, span_length=sp...]
    psum x1 -> x0, blocking collectives: 34.8 us -> none  [body(): d_kv_weight = lax.psum(wide_part, 'seq')]
    all_to_all x1, blocking collectives: 15.9 us -> 39.8 us  [swap(): return lax.all_to_all(array, 'seq', split_axis=0, concat_axis=0, tiled=True)]
    ppermute x0 -> x18, starting transfers between devices: none -> 23.6 us  [the longest x4 8.01 us: ring_sum(): from_high = lax.ppermute(third, 'nbr', minus)]
    reshape x4 -> x2, local copies, waits for them, and re-layouts: 17.9 us -> 2.13 us  [the longest x1 1.3 us: body(): pieces = database.reshape(stored, peers, piece, width).transpose(1, 0, 2, 3)]
    ppermute x0 -> x18, waiting for transfers between devices: none -> 14.6 us  [the longest x4 8.79 us: ring_sum(): from_low = lax.ppermute(first, 'nbr', plus)]
  transfers between devices with their start and end apart: 4 -> 24, of which waited for: 2 -> 12; matrix products, arithmetic and copies ran while one was open for 23% -> 4% of each run, Pallas kernels for 0% -> 2%
where the time goes in v1:
time: 245 us; the launch traced here: 243 us
  waiting for transfers between devices  85.4 us (35%)
  Pallas kernels  44.4 us (18%)
  starting transfers between devices  43.7 us (18%)
  blocking collectives  39.8 us (16%)
  between operations  14.4 us (6%)
  local copies, waits for them, and re-layouts  9.07 us (4%)
  other arithmetic  6.19 us (3%)
    all_to_all x5, waiting for transfers between devices, swap(): return lax.all_to_all(array, 'seq', split_axis=0, concat_axis=0, tiled=True)  70.2 us
    pallas_call x1, Pallas kernels, body(): pl.pallas_call(functools.partial(main_kernel, spans=spans, span_length=sp...  40.8 us
    all_to_all x1, blocking collectives, swap(): return lax.all_to_all(array, 'seq', split_axis=0, concat_axis=0, tiled=True)  39.8 us
    all_to_all x5, starting transfers between devices, swap(): return lax.all_to_all(array, 'seq', split_axis=0, concat_axis=0, tiled=True)  20 us
    ppermute x4, waiting for transfers between devices, ring_sum(): from_low = lax.ppermute(first, 'nbr', plus)  8.79 us
    ppermute x4, starting transfers between devices, ring_sum(): from_high = lax.ppermute(third, 'nbr', minus)  8.01 us
    ppermute x4, starting transfers between devices, ring_sum(): up = lax.ppermute(b[2][..., :half], 'nbr', plus)  6.45 us
  transfers between devices with their start and end apart: 24, of which 12 were waited for; matrix products, arithmetic and copies ran while one was open for 4% of the time, Pallas kernels for 2%

profile of v1, /device:TPU:2, one launch (start us, length us, event | category | flops | bytes accessed | tf_op | source)
XLA Modules:
  0.0 243.0 jit_solution(3314478407843481985)
XLA Ops:
  9.5 39.8 %all_to_all.30.stored_ref = bf16[8,72,1024]{2,1,0:T(8,128)(2,1)S(1)} all-to-all(bf16[8,72,1024]{2,1,0:T(8,128)(2,1)S(1)} %pad_maximum_fusion), channel_id=1, replica_groups=mesh['seq'=8,'nbr'=32] {'seq'}, dimensions={0} | all-to-all | bytes 2359296 | tf_op jit(solution)/shard_map/all_to_all | solution.py:154
  51.0 3.6 %all-to-all-start.1 = ((bf16[8,64,1024]{2,1,0:T(8,128)(2,1)}), bf16[8,64,1024]{2,1,0:T(8,128)(2,1)S(1)}, u32[]{:S(2)}, u32[]{:S(2)}) async-start(bf16[8,64,1024]{2,1,0:T(8,128)(2,1)} %pick.1), calls=%async_computation.1 | async-start | bytes 2097152 | tf_op jit(solution)/shard_map/all_to_all | solution.py:154
  54.6 27.5 %all-to-all-done.1 = bf16[8,64,1024]{2,1,0:T(8,128)(2,1)S(1)} async-done(((bf16[8,64,1024]{2,1,0:T(8,128)(2,1)}), bf16[8,64,1024]{2,1,0:T(8,128)(2,1)S(1)}, u32[]{:S(2)}, u32[]{:S(2)}) %all-to-all-start.1) | async-done | bytes 1048608 | tf_op jit(solution)/shard_map/all_to_all | solution.py:154
  84.2 40.8 %attend.1 = (bf16[128,2048]{1,0:T(8,128)(2,1)}, bf16[128,2048]{1,0:T(8,128)(2,1)}, bf16[16,32,2048]{2,1,0:T(8,128)(2,1)S(1)}, bf16[16,32,2048]{2,1,0:T(8,128)(2,...) custom-call(s32[1]{0:T(128)} %bitcast.core_ref, ...), custom_call_target="tpu_custom_call" | custom-call | flops 14000000000 | bytes 25165824 | tf_op jit(solution)/shard_map/attend/pallas_call | solution.py:203
  126.4 3.6 %all-to-all-start.4 = ((bf16[8,64,1024]{2,1,0:T(8,128)(2,1)}), bf16[8,64,1024]{2,1,0:T(8,128)(2,1)S(1)}, u32[]{:S(2)}, u32[]{:S(2)}) async-start(bf16[8,64,1024]{2,1,0:T(8,128)(2,1)} %bitcast.62), calls=%async_computation.4 | async-start | bytes 2097152 | tf_op jit(solution)/shard_map/all_to_all | solution.py:154
  130.4 2.4 add_convert_fusion.1
  135.1 2.4 add_convert_fusion
  137.7 1.7 collective-permute-start.10
  139.4 1.7 collective-permute-start.12
  141.5 1.7 collective-permute-start.2
  144.0 2.9 %collective-permute-done.10 = bf16[4,32,1024]{2,1,0:T(8,128)(2,1)S(1)} collective-permute-done((bf16[4,32,1024]{2,1,0:T(8,128)(2,1)S(1)}, bf16[4,32,1024]{2,1,0:T(8,128)(2,1)S(1)}, u32[]{:S(2)}, u32[]{:S(2)}) %collective-permute-start.10) | collective-permute-done | bytes 262176 | tf_op jit(solution)/shard_map/ppermute | solution.py:143
  147.4 3.0 %collective-permute-start.13 = (bf16[4,32,2048]{2,1,0:T(8,128)(2,1)S(1)}, bf16[4,32,2048]{2,1,0:T(8,128)(2,1)S(1)}, u32[]{:S(2)}, u32[]{:S(2)}) collective-permute-start(bf16[4,32,2048]{2,1,0:T(8,128)(2,1)S(1)} %pad_maximum_fusion.4), channel_id=1, source_target_pairs={{0,24},{1,25},{2,26},{3,27},{4,28},{5,29},{6,30},{7,31},{8,0},{9,1... | collective-permute-start | bytes 1572872 | tf_op jit(solution)/shard_map/ppermute | solution.py:148
  150.4 4.5 %collective-permute-done.2 = bf16[4,32,2048]{2,1,0:T(8,128)(2,1)S(1)} collective-permute-done((bf16[4,32,2048]{2,1,0:T(8,128)(2,1)S(1)}, bf16[4,32,2048]{2,1,0:T(8,128)(2,1)S(1)}, u32[]{:S(2)}, u32[]{:S(2)}) %collective-permute-start.2) | collective-permute-done | bytes 524320 | tf_op jit(solution)/shard_map/ppermute | solution.py:147
  156.6 1.7 collective-permute-start.5
  158.3 1.7 collective-permute-start.7
  164.6 2.8 %collective-permute-start.8 = (bf16[32,2048]{1,0:T(8,128)(2,1)S(1)}, bf16[32,2048]{1,0:T(8,128)(2,1)S(1)}, u32[]{:S(2)}, u32[]{:S(2)}) collective-permute-start(bf16[32,2048]{1,0:T(8,128)(2,1)S(1)} %pad_maximum_fusion.7), channel_id=1, source_target_pairs={{0,24},{1,25},{2,26},{3,27},{4,28},{5,29},{6,30},{7,31},{8,0},{9,1... | collective-permute-start | bytes 393224 | tf_op jit(solution)/shard_map/ppermute | solution.py:148
  170.7 2.7 %collective-permute-done.15 = bf16[32,2048]{1,0:T(8,128)(2,1)S(1)} collective-permute-done((bf16[32,2048]{1,0:T(8,128)(2,1)S(1)}, bf16[32,2048]{1,0:T(8,128)(2,1)S(1)}, u32[]{:S(2)}, u32[]{:S(2)}) %collective-permute-start.15) | collective-permute-done | bytes 131104 | tf_op jit(solution)/shard_map/ppermute | solution.py:147
  175.0 5.9 %all-to-all-start.2 = ((bf16[8,32,512]{2,1,0:T(8,128)(2,1)}), bf16[8,32,512]{2,1,0:T(8,128)(2,1)S(1)}, u32[]{:S(2)}, u32[]{:S(2)}) async-start(bf16[8,32,512]{2,1,0:T(8,128)(2,1)} %copy.22), calls=%async_computation.2 | async-start | bytes 524288 | tf_op jit(solution)/shard_map/all_to_all | solution.py:154
  180.9 2.0 add_rows.1
  182.9 8.4 %all-to-all-done.2 = bf16[8,32,512]{2,1,0:T(8,128)(2,1)S(1)} async-done(((bf16[8,32,512]{2,1,0:T(8,128)(2,1)}), bf16[8,32,512]{2,1,0:T(8,128)(2,1)S(1)}, u32[]{:S(2)}, u32[]{:S(2)}) %all-to-all-start.2) | async-done | bytes 262176 | tf_op jit(solution)/shard_map/all_to_all | solution.py:154
  191.4 3.6 %all-to-all-start.5 = ((bf16[8,64,1024]{2,1,0:T(8,128)(2,1)}), bf16[8,64,1024]{2,1,0:T(8,128)(2,1)S(1)}, u32[]{:S(2)}, u32[]{:S(2)}) async-start(bf16[8,64,1024]{2,1,0:T(8,128)(2,1)} %add_rows.1), calls=%async_computation.5 | async-start | bytes 2097152 | tf_op jit(solution)/shard_map/all_to_all | solution.py:154
  195.0 22.7 %all-to-all-done.5 = bf16[8,64,1024]{2,1,0:T(8,128)(2,1)S(1)} async-done(((bf16[8,64,1024]{2,1,0:T(8,128)(2,1)}), bf16[8,64,1024]{2,1,0:T(8,128)(2,1)S(1)}, u32[]{:S(2)}, u32[]{:S(2)}) %all-to-all-start.5) | async-done | bytes 1048608 | tf_op jit(solution)/shard_map/all_to_all | solution.py:154
  218.6 3.5 %all-to-all-start.3 = ((f32[8,32,512]{2,1,0:T(8,128)}), f32[8,32,512]{2,1,0:T(8,128)S(1)}, u32[]{:S(2)}, u32[]{:S(2)}) async-start(f32[8,32,512]{2,1,0:T(8,128)} %broadcast_in_dim.15), calls=%async_computation.3 | async-start | bytes 1048576 | tf_op jit(solution)/shard_map/all_to_all | solution.py:154
  223.8 11.5 %all-to-all-done.3 = f32[8,32,512]{2,1,0:T(8,128)S(1)} async-done(((f32[8,32,512]{2,1,0:T(8,128)}), f32[8,32,512]{2,1,0:T(8,128)S(1)}, u32[]{:S(2)}, u32[]{:S(2)}) %all-to-all-start.3) | async-done | bytes 524320 | tf_op jit(solution)/shard_map/all_to_all | solution.py:154
  (89 shorter events, 26.8 us)
Async XLA Ops:
  7.2 74.9 %all-gather.2.cloned.1.call-start = ((), (), s32[]{:S(2)}) async-start(), calls=%async_computation.6 | async-start | bytes 8650752 | tf_op jit(solution)/shard_map/all_gather | solution.py:172
  51.0 31.1 %all-to-all-start.1 = ((bf16[8,64,1024]{2,1,0:T(8,128)(2,1)}), bf16[8,64,1024]{2,1,0:T(8,128)(2,1)S(1)}, u32[]{:S(2)}, u32[]{:S(2)}) async-start(bf16[8,64,1024]{2,1,0:T(8,128)(2,1)} %pick.1), calls=%async_computation.1 | async-start | bytes 2097152 | tf_op jit(solution)/shard_map/all_to_all | solution.py:154
  125.9 4.5 %collective-permute-start = (bf16[16,32,2048]{2,1,0:T(8,128)(2,1)}, bf16[16,32,2048]{2,1,0:T(8,128)(2,1)}, u32[]{:S(2)}, u32[]{:S(2)}) collective-permute-start(bf16[16,32,2048]{2,1,0:T(8,128)(2,1)} %get-tuple-element.14), channel_id=1, source_target_pairs={{0,1},{1,0},{2,3},{3,2},{4,5},{5,4},{6,7},{7,6},{8,9},{9,8},{10,11... | collective-permute-start | bytes 6291464 | tf_op jit(solution)/shard_map/ppermute | solution.py:253
  125.9 9.2 %collective-permute-start.9 = (bf16[16,32,2048]{2,1,0:T(8,128)(2,1)}, bf16[16,32,2048]{2,1,0:T(8,128)(2,1)}, u32[]{:S(2)}, u32[]{:S(2)}) collective-permute-start(bf16[16,32,2048]{2,1,0:T(8,128)(2,1)} %get-tuple-element.16), channel_id=1, source_target_pairs={{0,1},{1,0},{2,3},{3,2},{4,5},{5,4},{6,7},{7,6},{8,9},{9,8},{10,11... | collective-permute-start | bytes 6291464 | tf_op jit(solution)/shard_map/ppermute | solution.py:254
  126.4 48.6 %all-to-all-start.4 = ((bf16[8,64,1024]{2,1,0:T(8,128)(2,1)}), bf16[8,64,1024]{2,1,0:T(8,128)(2,1)S(1)}, u32[]{:S(2)}, u32[]{:S(2)}) async-start(bf16[8,64,1024]{2,1,0:T(8,128)(2,1)} %bitcast.62), calls=%async_computation.4 | async-start | bytes 2097152 | tf_op jit(solution)/shard_map/all_to_all | solution.py:154
  133.0 8.4 %collective-permute-start.1 = (bf16[4,32,1024]{2,1,0:T(8,128)(2,1)S(1)}, bf16[4,32,1024]{2,1,0:T(8,128)(2,1)S(1)}, u32[]{:S(2)}, u32[]{:S(2)}) collective-permute-start(bf16[4,32,1024]{2,1,0:T(8,128)(2,1)S(1)} %get-tuple-element.29), channel_id=1, source_target_pairs={{0,2},{1,3},{2,4},{3,5},{4,6},{5,7},{6,0},{7,1},{8,10},{9,11},{10,... | collective-permute-start | bytes 786440 | tf_op jit(solution)/shard_map/ppermute | solution.py:143
  134.6 8.7 %collective-permute-start.3 = (bf16[4,32,1024]{2,1,0:T(8,128)(2,1)S(1)}, bf16[4,32,1024]{2,1,0:T(8,128)(2,1)S(1)}, u32[]{:S(2)}, u32[]{:S(2)}) collective-permute-start(bf16[4,32,1024]{2,1,0:T(8,128)(2,1)S(1)} %get-tuple-element.30), channel_id=1, source_target_pairs={{0,6},{1,7},{2,0},{3,1},{4,2},{5,3},{6,4},{7,5},{8,14},{9,15},{10,... | collective-permute-start | bytes 786440 | tf_op jit(solution)/shard_map/ppermute | solution.py:144
  137.7 9.1 %collective-permute-start.10 = (bf16[4,32,1024]{2,1,0:T(8,128)(2,1)S(1)}, bf16[4,32,1024]{2,1,0:T(8,128)(2,1)S(1)}, u32[]{:S(2)}, u32[]{:S(2)}) collective-permute-start(bf16[4,32,1024]{2,1,0:T(8,128)(2,1)S(1)} %get-tuple-element.38), channel_id=1, source_target_pairs={{0,8},{1,9},{2,10},{3,11},{4,12},{5,13},{6,14},{7,15},{8,16},{9,17... | collective-permute-start | bytes 786440 | tf_op jit(solution)/shard_map/ppermute | solution.py:143
  139.4 8.0 %collective-permute-start.12 = (bf16[4,32,1024]{2,1,0:T(8,128)(2,1)S(1)}, bf16[4,32,1024]{2,1,0:T(8,128)(2,1)S(1)}, u32[]{:S(2)}, u32[]{:S(2)}) collective-permute-start(bf16[4,32,1024]{2,1,0:T(8,128)(2,1)S(1)} %get-tuple-element.39), channel_id=1, source_target_pairs={{0,24},{1,25},{2,26},{3,27},{4,28},{5,29},{6,30},{7,31},{8,0},{9,1... | collective-permute-start | bytes 786440 | tf_op jit(solution)/shard_map/ppermute | solution.py:144
  141.5 13.4 %collective-permute-start.2 = (bf16[4,32,2048]{2,1,0:T(8,128)(2,1)S(1)}, bf16[4,32,2048]{2,1,0:T(8,128)(2,1)S(1)}, u32[]{:S(2)}, u32[]{:S(2)}) collective-permute-start(bf16[4,32,2048]{2,1,0:T(8,128)(2,1)S(1)} %pad_maximum_fusion.1), channel_id=1, source_target_pairs={{0,2},{1,3},{2,4},{3,5},{4,6},{5,7},{6,0},{7,1},{8,10},{9,11},{10,... | collective-permute-start | bytes 1572872 | tf_op jit(solution)/shard_map/ppermute | solution.py:147
  143.4 12.9 %collective-permute-start.4 = (bf16[4,32,2048]{2,1,0:T(8,128)(2,1)S(1)}, bf16[4,32,2048]{2,1,0:T(8,128)(2,1)S(1)}, u32[]{:S(2)}, u32[]{:S(2)}) collective-permute-start(bf16[4,32,2048]{2,1,0:T(8,128)(2,1)S(1)} %pad_maximum_fusion.2), channel_id=1, source_target_pairs={{0,6},{1,7},{2,0},{3,1},{4,2},{5,3},{6,4},{7,5},{8,14},{9,15},{10,... | collective-permute-start | bytes 1572872 | tf_op jit(solution)/shard_map/ppermute | solution.py:148
  146.9 14.6 %collective-permute-start.11 = (bf16[4,32,2048]{2,1,0:T(8,128)(2,1)S(1)}, bf16[4,32,2048]{2,1,0:T(8,128)(2,1)S(1)}, u32[]{:S(2)}, u32[]{:S(2)}) collective-permute-start(bf16[4,32,2048]{2,1,0:T(8,128)(2,1)S(1)} %pad_maximum_fusion.3), channel_id=1, source_target_pairs={{0,8},{1,9},{2,10},{3,11},{4,12},{5,13},{6,14},{7,15},{8,16},{9,17... | collective-permute-start | bytes 1572872 | tf_op jit(solution)/shard_map/ppermute | solution.py:147
  147.4 14.1 %collective-permute-start.13 = (bf16[4,32,2048]{2,1,0:T(8,128)(2,1)S(1)}, bf16[4,32,2048]{2,1,0:T(8,128)(2,1)S(1)}, u32[]{:S(2)}, u32[]{:S(2)}) collective-permute-start(bf16[4,32,2048]{2,1,0:T(8,128)(2,1)S(1)} %pad_maximum_fusion.4), channel_id=1, source_target_pairs={{0,24},{1,25},{2,26},{3,27},{4,28},{5,29},{6,30},{7,31},{8,0},{9,1... | collective-permute-start | bytes 1572872 | tf_op jit(solution)/shard_map/ppermute | solution.py:148
  156.6 7.3 %collective-permute-start.5 = (bf16[32,1024]{1,0:T(8,128)(2,1)S(1)}, bf16[32,1024]{1,0:T(8,128)(2,1)S(1)}, u32[]{:S(2)}, u32[]{:S(2)}) collective-permute-start(bf16[32,1024]{1,0:T(8,128)(2,1)S(1)} %get-tuple-element.44), channel_id=1, source_target_pairs={{0,8},{1,9},{2,10},{3,11},{4,12},{5,13},{6,14},{7,15},{8,16},{9,17... | collective-permute-start | bytes 196616 | tf_op jit(solution)/shard_map/ppermute | solution.py:143
  158.3 6.3 %collective-permute-start.7 = (bf16[32,1024]{1,0:T(8,128)(2,1)S(1)}, bf16[32,1024]{1,0:T(8,128)(2,1)S(1)}, u32[]{:S(2)}, u32[]{:S(2)}) collective-permute-start(bf16[32,1024]{1,0:T(8,128)(2,1)S(1)} %get-tuple-element.45), channel_id=1, source_target_pairs={{0,24},{1,25},{2,26},{3,27},{4,28},{5,29},{6,30},{7,31},{8,0},{9,1... | collective-permute-start | bytes 196616 | tf_op jit(solution)/shard_map/ppermute | solution.py:144
  161.8 5.6 %collective-permute-start.14 = (bf16[32,1024]{1,0:T(8,128)(2,1)S(1)}, bf16[32,1024]{1,0:T(8,128)(2,1)S(1)}, u32[]{:S(2)}, u32[]{:S(2)}) collective-permute-start(bf16[32,1024]{1,0:T(8,128)(2,1)S(1)} %get-tuple-element.50), channel_id=1, source_target_pairs={{0,2},{1,3},{2,4},{3,5},{4,6},{5,7},{6,0},{7,1},{8,10},{9,11},{10,... | collective-permute-start | bytes 196616 | tf_op jit(solution)/shard_map/ppermute | solution.py:143
  163.4 5.6 %collective-permute-start.16 = (bf16[32,1024]{1,0:T(8,128)(2,1)S(1)}, bf16[32,1024]{1,0:T(8,128)(2,1)S(1)}, u32[]{:S(2)}, u32[]{:S(2)}) collective-permute-start(bf16[32,1024]{1,0:T(8,128)(2,1)S(1)} %get-tuple-element.51), channel_id=1, source_target_pairs={{0,6},{1,7},{2,0},{3,1},{4,2},{5,3},{6,4},{7,5},{8,14},{9,15},{10,... | collective-permute-start | bytes 196616 | tf_op jit(solution)/shard_map/ppermute | solution.py:144
  164.0 6.7 %collective-permute-start.6 = (bf16[32,2048]{1,0:T(8,128)(2,1)S(1)}, bf16[32,2048]{1,0:T(8,128)(2,1)S(1)}, u32[]{:S(2)}, u32[]{:S(2)}) collective-permute-start(bf16[32,2048]{1,0:T(8,128)(2,1)S(1)} %pad_maximum_fusion.6), channel_id=1, source_target_pairs={{0,8},{1,9},{2,10},{3,11},{4,12},{5,13},{6,14},{7,15},{8,16},{9,17... | collective-permute-start | bytes 393224 | tf_op jit(solution)/shard_map/ppermute | solution.py:147
  164.6 6.0 %collective-permute-start.8 = (bf16[32,2048]{1,0:T(8,128)(2,1)S(1)}, bf16[32,2048]{1,0:T(8,128)(2,1)S(1)}, u32[]{:S(2)}, u32[]{:S(2)}) collective-permute-start(bf16[32,2048]{1,0:T(8,128)(2,1)S(1)} %pad_maximum_fusion.7), channel_id=1, source_target_pairs={{0,24},{1,25},{2,26},{3,27},{4,28},{5,29},{6,30},{7,31},{8,0},{9,1... | collective-permute-start | bytes 393224 | tf_op jit(solution)/shard_map/ppermute | solution.py:148
  167.4 6.0 %collective-permute-start.15 = (bf16[32,2048]{1,0:T(8,128)(2,1)S(1)}, bf16[32,2048]{1,0:T(8,128)(2,1)S(1)}, u32[]{:S(2)}, u32[]{:S(2)}) collective-permute-start(bf16[32,2048]{1,0:T(8,128)(2,1)S(1)} %pad_maximum_fusion.8), channel_id=1, source_target_pairs={{0,2},{1,3},{2,4},{3,5},{4,6},{5,7},{6,0},{7,1},{8,10},{9,11},{10,... | collective-permute-start | bytes 393224 | tf_op jit(solution)/shard_map/ppermute | solution.py:147
  169.0 5.0 %collective-permute-start.17 = (bf16[32,2048]{1,0:T(8,128)(2,1)S(1)}, bf16[32,2048]{1,0:T(8,128)(2,1)S(1)}, u32[]{:S(2)}, u32[]{:S(2)}) collective-permute-start(bf16[32,2048]{1,0:T(8,128)(2,1)S(1)} %pad_maximum_fusion.9), channel_id=1, source_target_pairs={{0,6},{1,7},{2,0},{3,1},{4,2},{5,3},{6,4},{7,5},{8,14},{9,15},{10,... | collective-permute-start | bytes 393224 | tf_op jit(solution)/shard_map/ppermute | solution.py:148
  175.0 16.3 %all-to-all-start.2 = ((bf16[8,32,512]{2,1,0:T(8,128)(2,1)}), bf16[8,32,512]{2,1,0:T(8,128)(2,1)S(1)}, u32[]{:S(2)}, u32[]{:S(2)}) async-start(bf16[8,32,512]{2,1,0:T(8,128)(2,1)} %copy.22), calls=%async_computation.2 | async-start | bytes 524288 | tf_op jit(solution)/shard_map/all_to_all | solution.py:154
  191.4 26.4 %all-to-all-start.5 = ((bf16[8,64,1024]{2,1,0:T(8,128)(2,1)}), bf16[8,64,1024]{2,1,0:T(8,128)(2,1)S(1)}, u32[]{:S(2)}, u32[]{:S(2)}) async-start(bf16[8,64,1024]{2,1,0:T(8,128)(2,1)} %add_rows.1), calls=%async_computation.5 | async-start | bytes 2097152 | tf_op jit(solution)/shard_map/all_to_all | solution.py:154
  218.6 16.7 %all-to-all-start.3 = ((f32[8,32,512]{2,1,0:T(8,128)}), f32[8,32,512]{2,1,0:T(8,128)S(1)}, u32[]{:S(2)}, u32[]{:S(2)}) async-start(f32[8,32,512]{2,1,0:T(8,128)} %broadcast_in_dim.15), calls=%async_computation.3 | async-start | bytes 1048576 | tf_op jit(solution)/shard_map/all_to_all | solution.py:154
  (7 other events, 42.2 us)
Sparse Core Ops, SparseCore 0:
  10.6 60.8 all-gather.1

commit v2 on v1

v2 whole, which is shorter than its diff:
```python
import functools

import jax
import jax.numpy as jnp
from jax import lax
from jax.experimental import pallas as pl
from jax.experimental.pallas import tpu as pltpu
from jax.sharding import PartitionSpec as P

HEAD_DIM = 128
K_NBR = 2
EPSILON = 1e-06
HEADS_STEP = 4
CHUNKS = 1
X_CHIPS = 4
Y_CHIPS = 4
F32 = jnp.float32
BF16 = jnp.bfloat16


def mm(a, b, ca, cb):
    return lax.dot_general(a, b, (((ca,), (cb,)), ((), ())), preferred_element_type=F32)


def pick_kernel(ids_ref, stored_ref, out_ref, *, peers, stored, requests, piece):
    for peer in range(peers):
        for r in range(requests):
            row = ids_ref[peer * requests + r]
            source = lax.div(row, stored)
            start = pl.multiple_of(lax.rem(row, stored) * piece, piece)
            out_ref[peer, pl.ds(r * piece, piece), :] = stored_ref[source, pl.ds(start, piece), :]


def sum_kernel(ids_ref, grads_ref, out_ref, total_ref, *, peers, requests, piece):
    total_ref[...] = jnp.zeros_like(total_ref)
    for peer in range(peers):
        for r in range(requests):
            row = ids_ref[peer * requests + r]
            total_ref[row] += grads_ref[peer, pl.ds(r * piece, piece), :].astype(F32)
    out_ref[...] = total_ref[...].astype(BF16).reshape(out_ref.shape)


def pair_kernel(at_ref, own_ref, got_ref, stay_ref, next_ref, prev_ref, up_ref, down_ref):
    half = up_ref.shape[0]

    def total(d):
        at = lax.rem(at_ref[0] + d, 4)
        return (own_ref[at].astype(F32) + got_ref[at].astype(F32)).astype(BF16)

    stay_ref[...] = total(0)
    next_ref[...] = total(1)
    prev_ref[...] = total(3)
    far = total(2)
    up_ref[...] = far[:half]
    down_ref[...] = far[half:]


def pair_call(at, own, got):
    ring, chips, rows, cols = own.shape
    width = 512
    whole = pl.BlockSpec((ring, chips, rows, width), lambda i: (0, 0, 0, i))
    block = pl.BlockSpec((chips, rows, width), lambda i: (0, 0, i))
    half = pl.BlockSpec((chips // 2, rows, width), lambda i: (0, 0, i))
    block_shape = jax.ShapeDtypeStruct((chips, rows, cols), BF16)
    half_shape = jax.ShapeDtypeStruct((chips // 2, rows, cols), BF16)
    return pl.pallas_call(
        pair_kernel,
        grid=(cols // width,),
        out_shape=[block_shape] * 3 + [half_shape] * 2,
        in_specs=[pl.BlockSpec(memory_space=pltpu.SMEM), whole, whole],
        out_specs=[block] * 3 + [half] * 2,
        compiler_params=pltpu.CompilerParams(vmem_limit_bytes=58 << 20),
        cost_estimate=pl.CostEstimate(flops=0, bytes_accessed=1 << 10, transcendentals=0),
        name="pair_add",
    )(at, own, got)


def main_kernel(*refs, spans, span_length, chunk):
    core_ref, rows_ref, gain_ref, wk_ref, wv_ref, q_ref, g_ref = refs[:7]
    normed_ref, normed_t_ref, dnormed_ref, dk_ref, dv_ref = refs[-5:]
    ctx_ref, dq_ref, own_ref, oth_ref, final_ref = refs[-10:-5]
    step = pl.program_id(0)
    scale_factor = HEAD_DIM ** (-0.5)
    positions = normed_ref.shape[0] // spans
    width = rows_ref.shape[-1]
    gain = gain_ref[...]

    def wide_rows(c):
        return rows_ref[:, c].astype(F32).reshape(positions, width)

    @pl.when(step == 0)
    def _():
        for c in range(spans):
            x = wide_rows(c)
            r = lax.rsqrt(jnp.mean(x * x, axis=-1, keepdims=True) + EPSILON)
            normed = (x * r * gain).astype(BF16)
            normed_ref[pl.ds(c * positions, positions), :] = normed
            normed_t_ref[:, pl.ds(c * positions, positions)] = normed.T
        if chunk:
            dnormed_ref[...] = refs[7][...]
        else:
            dnormed_ref[...] = jnp.zeros_like(dnormed_ref)

    normed = normed_ref[...]
    keys = mm(normed, wk_ref[...], 1, 0).astype(BF16)
    values = mm(normed, wv_ref[...], 1, 0).astype(BF16)
    blocks = [
        (
            slice(c * span_length, (c + 1) * span_length),
            slice(c * positions, (c + 1) * positions),
            slice(h * HEAD_DIM, (h + 1) * HEAD_DIM),
        )
        for c in range(spans)
        for h in range(HEADS_STEP)
    ]
    scores = jnp.concatenate(
        [mm(q_ref[toks, cols], keys[poss, cols], 1, 1) for toks, poss, cols in blocks], axis=0
    )
    d_probs = jnp.concatenate(
        [mm(g_ref[toks, cols], values[poss, cols], 1, 1) for toks, poss, cols in blocks], axis=0
    )
    scores = scores * scale_factor
    expanded = jnp.exp(scores - jnp.max(scores, axis=-1, keepdims=True))
    probs = expanded * (1.0 / jnp.sum(expanded, axis=-1, keepdims=True))
    delta = jnp.sum(probs * d_probs, axis=-1, keepdims=True)
    probs_half = probs.astype(BF16)
    d_scores = (probs * (d_probs - delta) * scale_factor).astype(BF16)
    for n, (toks, poss, cols) in enumerate(blocks):
        own = slice(n * span_length, (n + 1) * span_length)
        ctx_ref[toks, cols] = mm(probs_half[own], values[poss, cols], 1, 0).astype(BF16)
        dq_ref[toks, cols] = mm(d_scores[own], keys[poss, cols], 1, 0).astype(BF16)
        dk_ref[poss, cols] = mm(d_scores[own], q_ref[toks, cols], 0, 0).astype(BF16)
        dv_ref[poss, cols] = mm(probs_half[own], g_ref[toks, cols], 0, 0).astype(BF16)
    dk = dk_ref[...]
    dv = dv_ref[...]
    dnormed_ref[...] += mm(dk, wk_ref[...], 1, 1) + mm(dv, wv_ref[...], 1, 1)
    rows, cols = own_ref.shape[-2:]
    for kind, grad in enumerate((dk, dv)):
        term = mm(normed_t_ref[...], grad, 1, 0).astype(BF16)
        term = term.reshape(Y_CHIPS, X_CHIPS, rows, cols)

        def put(ref):
            for y in range(Y_CHIPS):
                for x in range(X_CHIPS):
                    at = (x, y) if kind == 0 else (y, x)
                    ref[at] = term[y, x]

        @pl.when(core_ref[0] == kind)
        def _():
            put(own_ref)

        @pl.when(core_ref[0] != kind)
        def _():
            put(oth_ref)

    @pl.when(step == pl.num_programs(0) - 1)
    def _():
        if chunk < CHUNKS - 1:
            final_ref[...] = dnormed_ref[...]
            return
        for c in range(spans):
            x = wide_rows(c)
            r = lax.rsqrt(jnp.mean(x * x, axis=-1, keepdims=True) + EPSILON)
            dng = dnormed_ref[pl.ds(c * positions, positions), :] * gain
            inner = jnp.sum(dng * x, axis=-1, keepdims=True)
            dx = r * dng - x * (r * r * r * inner * (1.0 / width))
            final_ref[:, c] = dx.astype(BF16).reshape(final_ref.shape[0], *final_ref.shape[2:])


def attend_call(core, rows, gain, weight, queries, d_context, chunk, carried):
    peers, spans, run, width = rows.shape
    tokens = peers * spans * run
    span_length = queries.shape[0] // spans
    kv_width = queries.shape[1]
    step_cols = HEADS_STEP * HEAD_DIM
    steps = kv_width // (CHUNKS * step_cols)
    at = chunk * steps
    half = (X_CHIPS, Y_CHIPS, width // (X_CHIPS * Y_CHIPS))
    half_shape = jax.ShapeDtypeStruct((*half, kv_width // CHUNKS), BF16)
    half_spec = pl.BlockSpec((*half, step_cols), lambda i: (0, 0, 0, i))
    token_shape = jax.ShapeDtypeStruct(queries.shape, BF16)
    token_spec = pl.BlockSpec((queries.shape[0], step_cols), lambda i: (0, at + i))
    whole = pl.BlockSpec(rows.shape, lambda i: (0, 0, 0, 0))
    wide_spec = pl.BlockSpec((tokens, width), lambda i: (0, 0))
    last = chunk == CHUNKS - 1
    any_spec = pl.BlockSpec(memory_space=pl.ANY)
    more = [] if chunk == 0 else list(carried)
    return pl.pallas_call(
        functools.partial(main_kernel, spans=spans, span_length=span_length, chunk=chunk),
        grid=(steps,),
        out_shape=[
            token_shape,
            token_shape,
            half_shape,
            half_shape,
            jax.ShapeDtypeStruct(rows.shape, BF16)
            if last
            else jax.ShapeDtypeStruct((tokens, width), F32),
        ],
        in_specs=[
            pl.BlockSpec(memory_space=pltpu.SMEM),
            whole,
            pl.BlockSpec((1, width), lambda i: (0, 0)),
            pl.BlockSpec((width, step_cols), lambda i: (0, at + i)),
            pl.BlockSpec((width, step_cols), lambda i: (0, CHUNKS * steps + at + i)),
            token_spec,
            token_spec,
        ]
        + ([wide_spec, any_spec, any_spec] if more else []),
        out_specs=[token_spec, token_spec, half_spec, half_spec, whole if last else wide_spec],
        scratch_shapes=[
            pltpu.VMEM((tokens, width), BF16),
            pltpu.VMEM((width, tokens), BF16),
            pltpu.VMEM((tokens, width), F32),
            pltpu.VMEM((tokens, step_cols), BF16),
            pltpu.VMEM((tokens, step_cols), BF16),
        ],
        input_output_aliases={8: 0, 9: 1} if more else {},
        compiler_params=pltpu.CompilerParams(vmem_limit_bytes=58 << 20),
        cost_estimate=pl.CostEstimate(
            flops=14_000_000_000 // CHUNKS,
            bytes_accessed=24 << 20,
            transcendentals=(1 << 20) // CHUNKS,
        ),
        name="attend",
    )(core, rows, gain, weight, weight, queries, d_context, *more)


def ring_sum(blocks, position, plus, minus):
    b = [
        lax.dynamic_index_in_dim(blocks, (position + d) % 4, 0, keepdims=False) for d in range(4)
    ]
    half = b[0].shape[0] // 2
    up = lax.ppermute(b[2][:half], "nbr", plus)
    down = lax.ppermute(b[2][half:], "nbr", minus)
    first = lax.dynamic_update_slice(b[1], b[1][:half] + up, (0,) * b[1].ndim)
    third = lax.dynamic_update_slice(b[3], b[3][half:] + down, (half,) + (0,) * (b[3].ndim - 1))
    from_low = lax.ppermute(first, "nbr", plus)
    from_high = lax.ppermute(third, "nbr", minus)
    total = b[0].astype(F32) + from_low.astype(F32) + from_high.astype(F32)
    return total.astype(BF16)


def swap(array):
    return lax.all_to_all(array, "seq", split_axis=0, concat_axis=0, tiled=True)


def body(queries, d_context, database, neighbour_source, neighbour_slot, enc_gain, kv_weight):
    peers = lax.axis_size("seq")
    spans = neighbour_source.shape[0]
    requests = spans * K_NBR
    stored, row_length, width = database.shape
    piece = row_length // peers
    kv_width = kv_weight.shape[1] // 2
    me = lax.axis_index("nbr")
    core = me % 2
    x_at = (me // 2) % X_CHIPS
    y_at = me // (2 * X_CHIPS)
    chips = X_CHIPS * Y_CHIPS
    shard_rows = kv_weight.shape[0]

    weight_full = lax.all_gather(kv_weight, "nbr", axis=0, tiled=True)

    wanted = (neighbour_source * stored + neighbour_slot).reshape(1, 1, requests)
    note = jnp.pad(wanted.astype(BF16), ((0, 0), (0, 7), (0, width - requests)))
    note = jnp.broadcast_to(note, (peers, 8, width))
    pieces = database.reshape(stored, peers, piece, width).transpose(1, 0, 2, 3)
    pieces = pieces.reshape(peers, stored * piece, width)
    held = swap(jnp.concatenate([pieces, note], axis=1))
    ids = held[:, stored * piece, :requests].astype(jnp.int32).reshape(peers * requests)
    ids = jnp.clip(ids, 0, peers * stored - 1)

    smem = pl.BlockSpec(memory_space=pltpu.SMEM)
    vmem = pl.BlockSpec(memory_space=pltpu.VMEM)
    picked = pl.pallas_call(
        functools.partial(pick_kernel, peers=peers, stored=stored, requests=requests, piece=piece),
        out_shape=jax.ShapeDtypeStruct((peers, requests * piece, width), BF16),
        in_specs=[smem, vmem],
        out_specs=vmem,
        compiler_params=pltpu.CompilerParams(vmem_limit_bytes=16 << 20),
        cost_estimate=pl.CostEstimate(flops=0, bytes_accessed=4 << 20, transcendentals=0),
        name="pick",
    )(ids, held)
    rows = swap(picked).reshape(peers, spans, K_NBR * piece, width)

    gain = enc_gain.reshape(1, width)
    core_ref = core.reshape(1)
    carried, owns, oths = None, [], []
    for chunk in range(CHUNKS):
        context, d_queries, own, oth, carry = attend_call(
            core_ref, rows, gain, weight_full, queries, d_context, chunk, carried
        )
        owns.append(own)
        oths.append(oth)
        carried = (carry, context, d_queries)

    returned = swap(carry.reshape(peers, requests * piece, width))

    pair = [(i, i ^ 1) for i in range(2 * chips)]

    def shifted(stage, by):
        moves = []
        for y in range(Y_CHIPS):
            for x in range(X_CHIPS):
                for k in range(2):
                    if (k + stage) % 2 == 0:
                        to_chip = y * X_CHIPS + (x + by) % X_CHIPS
                    else:
                        to_chip = ((y + by) % Y_CHIPS) * X_CHIPS + x
                    moves.append(((y * X_CHIPS + x) * 2 + k, to_chip * 2 + k))
        return moves

    first_at = jnp.where(core == 0, x_at, y_at)
    second_at = jnp.where(core == 0, y_at, x_at)
    plus, minus = shifted(0, 1), shifted(0, -1)
    got = lax.ppermute(oth, "nbr", pair)
    stay, ahead, behind, up, down = pair_call(first_at.reshape(1), own, got)
    half = up.shape[0]
    up = lax.ppermute(up, "nbr", plus)
    down = lax.ppermute(down, "nbr", minus)
    ahead = lax.dynamic_update_slice(ahead, ahead[:half] + up, (0, 0, 0))
    behind = lax.dynamic_update_slice(behind, behind[half:] + down, (half, 0, 0))

    summed = pl.pallas_call(
        functools.partial(sum_kernel, peers=peers, requests=requests, piece=piece),
        out_shape=jax.ShapeDtypeStruct((peers, stored * piece, width), BF16),
        in_specs=[smem, vmem],
        out_specs=vmem,
        scratch_shapes=[pltpu.VMEM((peers * stored, piece, width), F32)],
        compiler_params=pltpu.CompilerParams(vmem_limit_bytes=16 << 20),
        cost_estimate=pl.CostEstimate(flops=0, bytes_accessed=4 << 20, transcendentals=0),
        name="add_rows",
    )(ids, returned)
    low = lax.ppermute(ahead, "nbr", plus)
    high = lax.ppermute(behind, "nbr", minus)
    part = (stay.astype(F32) + low.astype(F32) + high.astype(F32)).astype(BF16)
    part, summed = lax.optimization_barrier((part, summed))
    final = swap(summed)
    part = ring_sum(part, second_at, shifted(1, 1), shifted(1, -1))

    part = part.reshape(2, shard_rows, kv_width)
    keep = lax.dynamic_index_in_dim(part, core, 0, keepdims=False)
    give = lax.dynamic_index_in_dim(part, 1 - core, 0, keepdims=False)
    got = lax.ppermute(give, "nbr", pair)
    keep, got, final = lax.optimization_barrier((keep, got, final))
    final = final.reshape(peers, stored, piece, width)
    d_database = final.transpose(1, 0, 2, 3).reshape(database.shape).astype(F32)

    first = jnp.where(core == 0, keep, got).reshape(peers // 2, -1, kv_width)
    second = jnp.where(core == 0, got, keep).reshape(peers // 2, -1, kv_width)
    terms = swap(jnp.concatenate([first, second], axis=0))
    total = jnp.sum(terms.astype(F32), axis=0, keepdims=True).astype(BF16)
    totals = swap(jnp.broadcast_to(total, terms.shape)).astype(F32)
    totals = totals.reshape(2, shard_rows, kv_width)
    d_kv_weight = jnp.concatenate([totals[0], totals[1]], axis=1)
    return context, d_queries, d_kv_weight, d_database


def solution(mesh):
    return jax.shard_map(
        body,
        mesh=mesh,
        in_specs=(
            P(("seq", "nbr"), None),
            P(("seq", "nbr"), None),
            P(("seq", "nbr"), None, None),
            P(("seq", "nbr"), None),
            P(("seq", "nbr"), None),
            P(),
            P("nbr", None),
        ),
        out_specs=(
            P(("seq", "nbr"), None),
            P(("seq", "nbr"), None),
            P("nbr", None),
            P(("seq", "nbr"), None, None),
        ),
        check_vma=False,
    )
```

time: 245 us -> 235 us (0.959)
  starting transfers between devices: 43.7 us -> 25.2 us
  blocking collectives: 39.8 us -> 54.6 us
  Pallas kernels: 44.4 us -> 35 us
  waiting for transfers between devices: 85.4 us -> 92 us
  local copies, waits for them, and re-layouts: 9.07 us -> 4.78 us
    all_to_all x1 -> x2, blocking collectives: 39.8 us -> 54.6 us  [swap(): return lax.all_to_all(array, 'seq', split_axis=0, concat_axis=0, tiled=True)]
    ppermute x10 -> x8, waiting for transfers between devices: 3.71 us -> 15.5 us  [the longest x1 7.44 us: body(): got = lax.ppermute(oth, 'nbr', pair)]
    pallas_call x1 -> x2, Pallas kernels: 40.8 us -> 31.3 us  [the longest x1 25.4 us: attend_call(): pl.pallas_call(functools.partial(main_kernel, spans=spans, span_length=sp...]
    all_to_all x5 -> x4, starting transfers between devices: 20 us -> 14.1 us  [swap(): return lax.all_to_all(array, 'seq', split_axis=0, concat_axis=0, tiled=True)]
    ppermute x4 -> x1, waiting for transfers between devices: 8.79 us -> 3.69 us  [ring_sum(): from_low = lax.ppermute(first, 'nbr', plus)]
    ppermute x4 -> x1, starting transfers between devices: 8.01 us -> 3.31 us  [ring_sum(): from_high = lax.ppermute(third, 'nbr', minus)]
    ppermute x4 -> x1, starting transfers between devices: 4.29 us -> 0.01 us  [ring_sum(): from_low = lax.ppermute(first, 'nbr', plus)]
    dynamic_update_slice x0 -> x3, other arithmetic: none -> 4.18 us  [the longest x1 2.13 us: body(): ahead = lax.dynamic_update_slice(ahead, ahead[:half] + up, (0, 0, 0))]
  transfers between devices with their start and end apart: 24 -> 15, of which waited for: 12 -> 10; matrix products, arithmetic and copies ran while one was open for 4% -> 4% of each run, Pallas kernels for 2% -> 2%
where the time goes in v2:
time: 235 us; the launch traced here: 234 us
  waiting for transfers between devices  92 us (39%)
  blocking collectives  54.6 us (23%)
  Pallas kernels  35 us (15%)
  starting transfers between devices  25.2 us (11%)
  between operations  14.2 us (6%)
  other arithmetic  8.05 us (3%)
  local copies, waits for them, and re-layouts  4.78 us (2%)
    all_to_all x4, waiting for transfers between devices, swap(): return lax.all_to_all(array, 'seq', split_axis=0, concat_axis=0, tiled=True)  68.2 us
    all_to_all x2, blocking collectives, swap(): return lax.all_to_all(array, 'seq', split_axis=0, concat_axis=0, tiled=True)  54.6 us
    pallas_call x1, Pallas kernels, attend_call(): pl.pallas_call(functools.partial(main_kernel, spans=spans, span_length=sp...  25.4 us
    all_to_all x4, starting transfers between devices, swap(): return lax.all_to_all(array, 'seq', split_axis=0, concat_axis=0, tiled=True)  14.1 us
    ppermute x1, waiting for transfers between devices, body(): got = lax.ppermute(oth, 'nbr', pair)  7.44 us
    pallas_call x1, Pallas kernels, pair_call(): pl.pallas_call(pair_kernel, grid=(cols // width,), out_shape=[block_shape...  5.91 us
  transfers between devices with their start and end apart: 15, of which 10 were waited for; matrix products, arithmetic and copies ran while one was open for 4% of the time, Pallas kernels for 2%

profile of v2, /device:TPU:2, one launch (start us, length us, event | category | flops | bytes accessed | tf_op | source)
XLA Modules:
  0.0 233.8 jit_solution(14189416040426285866)
XLA Ops:
  10.2 39.8 %all_to_all.30.stored_ref = bf16[8,72,1024]{2,1,0:T(8,128)(2,1)S(1)} all-to-all(bf16[8,72,1024]{2,1,0:T(8,128)(2,1)S(1)} %pad_maximum_fusion), channel_id=1, replica_groups=mesh['seq'=8,'nbr'=32] {'seq'}, dimensions={0} | all-to-all | bytes 2359296 | tf_op jit(solution)/shard_map/all_to_all | solution.py:245
  50.1 1.6 pick.1
  51.7 3.6 %all-to-all-start.1 = ((bf16[8,64,1024]{2,1,0:T(8,128)(2,1)}), bf16[8,64,1024]{2,1,0:T(8,128)(2,1)S(1)}, u32[]{:S(2)}, u32[]{:S(2)}) async-start(bf16[8,64,1024]{2,1,0:T(8,128)(2,1)} %pick.1), calls=%async_computation.1 | async-start | bytes 2097152 | tf_op jit(solution)/shard_map/all_to_all | solution.py:245
  55.3 27.5 %all-to-all-done.1 = bf16[8,64,1024]{2,1,0:T(8,128)(2,1)S(1)} async-done(((bf16[8,64,1024]{2,1,0:T(8,128)(2,1)}), bf16[8,64,1024]{2,1,0:T(8,128)(2,1)S(1)}, u32[]{:S(2)}, u32[]{:S(2)}) %all-to-all-start.1) | async-done | bytes 1048608 | tf_op jit(solution)/shard_map/all_to_all | solution.py:245
  83.7 25.4 %attend.1 = (bf16[128,2048]{1,0:T(8,128)(2,1)}, bf16[128,2048]{1,0:T(8,128)(2,1)}, bf16[4,4,64,2048]{3,2,1,0:T(8,128)(2,1)}, bf16[4,4,64,2048]{3,2,1,0:T(8,128)(2,1)}, bf16[8,2,32,1024]{3,2,1,0:T(8,128)(2,1)}) custom-call(s32[1]{0:T(128)} %bitcast.refs_0_, bf16[8,2,32,1024]{3,2,1,0:T(8,128)(2,1)} %bitcast.56, f32[1,1024]{1,0:T(1,128)} %bitcast.58, ...), custom_call_target="tpu_custom_call" | custom-call | flops 14000000000 | bytes 25165824 | tf_op jit(solution)/shard_map/attend/pallas_call | solution.py:188
  109.3 7.4 %collective-permute-done.got_ref = bf16[4,4,64,2048]{3,2,1,0:T(8,128)(2,1)} collective-permute-done((bf16[4,4,64,2048]{3,2,1,0:T(8,128)(2,1)}, bf16[4,4,64,2048]{3,2,1,0:T(8,128)(2,1)}, u32[]{:S(2)}, u32[]{:S(2)}) %collective-permute-start) | collective-permute-done | bytes 4194336 | tf_op jit(solution)/shard_map/ppermute | solution.py:316
  116.7 5.9 %pair_add.1 = (bf16[4,64,2048]{2,1,0:T(8,128)(2,1)}, bf16[4,64,2048]{2,1,0:T(8,128)(2,1)}, bf16[4,64,2048]{2,1,0:T(8,128)(2,1)}, bf16[2,64,2048]{2,1,0:T(8,128)(2,1)}, bf16[2,64,2048]{2,1,0:T(8,128)(2,1)}) custom-call(s32[1]{0:T(128)} %bitcast.7.at_ref, bf16[4,4,64,2048]{3,2,1,0:T(8,128)(2,1)} %get-tuple-element.21.own_ref, ...), custom_call_target="tpu_custom_call" | custom-call | bytes 1024 | tf_op jit(solution)/shard_map/pair_add/pallas_call | solution.py:66
  124.7 3.6 %all-to-all-start.2 = ((bf16[8,64,1024]{2,1,0:T(8,128)(2,1)}), bf16[8,64,1024]{2,1,0:T(8,128)(2,1)S(1)}, u32[]{:S(2)}, u32[]{:S(2)}) async-start(bf16[8,64,1024]{2,1,0:T(8,128)(2,1)} %bitcast.8), calls=%async_computation.2 | async-start | bytes 2097152 | tf_op jit(solution)/shard_map/all_to_all | solution.py:245
  128.3 3.8 %collective-permute-done.3 = bf16[2,64,2048]{2,1,0:T(8,128)(2,1)S(1)} collective-permute-done((bf16[2,64,2048]{2,1,0:T(8,128)(2,1)}, bf16[2,64,2048]{2,1,0:T(8,128)(2,1)S(1)}, u32[]{:S(2)}, u32[]{:S(2)}) %collective-permute-start.3) | collective-permute-done | bytes 524320 | tf_op jit(solution)/shard_map/ppermute | solution.py:320
  132.1 2.0 add_dynamic-update-slice_fusion
  135.0 2.1 add_dynamic-update-slice_fusion.1
  138.2 20.1 %all-to-all-done.2.grads_ref = bf16[8,64,1024]{2,1,0:T(8,128)(2,1)S(1)} async-done(((bf16[8,64,1024]{2,1,0:T(8,128)(2,1)}), bf16[8,64,1024]{2,1,0:T(8,128)(2,1)S(1)}, u32[]{:S(2)}, u32[]{:S(2)}) %all-to-all-start.2) | async-done | bytes 1048608 | tf_op jit(solution)/shard_map/all_to_all | solution.py:245
  158.3 2.0 add_rows.1
  160.4 1.7 add_convert_fusion
  162.1 3.6 %all-to-all-start.3 = ((bf16[8,64,1024]{2,1,0:T(8,128)(2,1)}), bf16[8,64,1024]{2,1,0:T(8,128)(2,1)S(1)}, u32[]{:S(2)}, u32[]{:S(2)}) async-start(bf16[8,64,1024]{2,1,0:T(8,128)(2,1)} %add_rows.1), calls=%async_computation.3 | async-start | bytes 2097152 | tf_op jit(solution)/shard_map/all_to_all | solution.py:245
  166.2 3.1 %collective-permute-start.7 = (bf16[32,2048]{1,0:T(8,128)(2,1)S(1)}, bf16[32,2048]{1,0:T(8,128)(2,1)S(1)}, u32[]{:S(2)}, u32[]{:S(2)}) collective-permute-start(bf16[32,2048]{1,0:T(8,128)(2,1)S(1)} %get-tuple-element.37), channel_id=1, source_target_pairs={{0,24},{1,7},{2,26},{3,1},{4,28},{5,3},{6,30},{7,5},{8,0},{9,15},{... | collective-permute-start | bytes 393224 | tf_op jit(solution)/shard_map/ppermute | solution.py:235
  169.3 2.9 %collective-permute-done.5 = bf16[32,2048]{1,0:T(8,128)(2,1)S(1)} collective-permute-done((bf16[32,2048]{1,0:T(8,128)(2,1)S(1)}, bf16[32,2048]{1,0:T(8,128)(2,1)S(1)}, u32[]{:S(2)}, u32[]{:S(2)}) %collective-permute-start.5) | collective-permute-done | bytes 131104 | tf_op jit(solution)/shard_map/ppermute | solution.py:234
  172.2 3.3 %collective-permute-start.8 = (bf16[64,2048]{1,0:T(8,128)(2,1)S(1)}, bf16[64,2048]{1,0:T(8,128)(2,1)S(1)}, u32[]{:S(2)}, u32[]{:S(2)}) collective-permute-start(bf16[64,2048]{1,0:T(8,128)(2,1)S(1)} %get-tuple-element.35), channel_id=1, source_target_pairs={{0,24},{1,7},{2,26},{3,1},{4,28},{5,3},{6,30},{7,5},{8,0},{9,15},{... | collective-permute-start | bytes 786440 | tf_op jit(solution)/shard_map/ppermute | solution.py:239
  175.6 3.9 %collective-permute-done.8 = bf16[64,2048]{1,0:T(8,128)(2,1)S(1)} collective-permute-done((bf16[64,2048]{1,0:T(8,128)(2,1)S(1)}, bf16[64,2048]{1,0:T(8,128)(2,1)S(1)}, u32[]{:S(2)}, u32[]{:S(2)}) %collective-permute-start.8) | collective-permute-done | bytes 262176 | tf_op jit(solution)/shard_map/ppermute | solution.py:239
  179.4 3.7 %collective-permute-done.6 = bf16[64,2048]{1,0:T(8,128)(2,1)S(1)} collective-permute-done((bf16[64,2048]{1,0:T(8,128)(2,1)S(1)}, bf16[64,2048]{1,0:T(8,128)(2,1)S(1)}, u32[]{:S(2)}, u32[]{:S(2)}) %collective-permute-start.6) | collective-permute-done | bytes 262176 | tf_op jit(solution)/shard_map/ppermute | solution.py:238
  184.7 10.2 %all-to-all-done.3 = bf16[8,64,1024]{2,1,0:T(8,128)(2,1)S(1)} async-done(((bf16[8,64,1024]{2,1,0:T(8,128)(2,1)}), bf16[8,64,1024]{2,1,0:T(8,128)(2,1)S(1)}, u32[]{:S(2)}, u32[]{:S(2)}) %all-to-all-start.3) | async-done | bytes 1048608 | tf_op jit(solution)/shard_map/all_to_all | solution.py:245
  195.0 14.8 %all_to_all.31 = bf16[8,8,2048]{2,1,0:T(8,128)(2,1)S(1)} all-to-all(bf16[8,8,2048]{2,1,0:T(8,128)(2,1)S(1)} %pad_maximum_fusion.2), channel_id=1, replica_groups=mesh['seq'=8,'nbr'=32] {'seq'}, dimensions={0} | all-to-all | bytes 524288 | tf_op jit(solution)/shard_map/all_to_all | solution.py:245
  210.5 3.4 %all-to-all-start.5 = ((bf16[8,8,2048]{2,1,0:T(8,128)(2,1)}), bf16[8,8,2048]{2,1,0:T(8,128)(2,1)S(1)}, u32[]{:S(2)}, u32[]{:S(2)}) async-start(bf16[8,8,2048]{2,1,0:T(8,128)(2,1)} %broadcast_in_dim.15), calls=%async_computation.5 | async-start | bytes 524288 | tf_op jit(solution)/shard_map/all_to_all | solution.py:245
  215.6 10.4 %all-to-all-done.5 = bf16[8,8,2048]{2,1,0:T(8,128)(2,1)S(1)} async-done(((bf16[8,8,2048]{2,1,0:T(8,128)(2,1)}), bf16[8,8,2048]{2,1,0:T(8,128)(2,1)S(1)}, u32[]{:S(2)}, u32[]{:S(2)}) %all-to-all-start.5) | async-done | bytes 262176 | tf_op jit(solution)/shard_map/all_to_all | solution.py:245
  (42 shorter events, 13.8 us)
Async XLA Ops:
  7.2 75.6 %all-gather.2.cloned.1.call-start = ((), (), s32[]{:S(2)}) async-start(), calls=%async_computation.6 | async-start | bytes 8650752 | tf_op jit(solution)/shard_map/all_gather | solution.py:262
  51.7 31.1 %all-to-all-start.1 = ((bf16[8,64,1024]{2,1,0:T(8,128)(2,1)}), bf16[8,64,1024]{2,1,0:T(8,128)(2,1)S(1)}, u32[]{:S(2)}, u32[]{:S(2)}) async-start(bf16[8,64,1024]{2,1,0:T(8,128)(2,1)} %pick.1), calls=%async_computation.1 | async-start | bytes 2097152 | tf_op jit(solution)/shard_map/all_to_all | solution.py:245
  82.8 1.0 copy-start
  109.2 7.6 %collective-permute-start = (bf16[4,4,64,2048]{3,2,1,0:T(8,128)(2,1)}, bf16[4,4,64,2048]{3,2,1,0:T(8,128)(2,1)}, u32[]{:S(2)}, u32[]{:S(2)}) collective-permute-start(bf16[4,4,64,2048]{3,2,1,0:T(8,128)(2,1)} %get-tuple-element.22), channel_id=1, source_target_pairs={{0,1},{1,0},{2,3},{3,2},{4,5},{5,4},{6,7},{7,6},{8,9},{9,8},{10,11... | collective-permute-start | bytes 12582920 | tf_op jit(solution)/shard_map/ppermute | solution.py:316
  122.7 9.4 %collective-permute-start.3 = (bf16[2,64,2048]{2,1,0:T(8,128)(2,1)}, bf16[2,64,2048]{2,1,0:T(8,128)(2,1)S(1)}, u32[]{:S(2)}, u32[]{:S(2)}) collective-permute-start(bf16[2,64,2048]{2,1,0:T(8,128)(2,1)} %get-tuple-element.27), channel_id=1, source_target_pairs={{0,6},{1,25},{2,0},{3,27},{4,2},{5,29},{6,4},{7,31},{8,14},{9,1},{... | collective-permute-start | bytes 1572872 | tf_op jit(solution)/shard_map/ppermute | solution.py:320
  123.2 11.8 %collective-permute-start.1 = (bf16[2,64,2048]{2,1,0:T(8,128)(2,1)}, bf16[2,64,2048]{2,1,0:T(8,128)(2,1)}, u32[]{:S(2)}, u32[]{:S(2)}) collective-permute-start(bf16[2,64,2048]{2,1,0:T(8,128)(2,1)} %get-tuple-element.25), channel_id=1, source_target_pairs={{0,2},{1,9},{2,4},{3,11},{4,6},{5,13},{6,0},{7,15},{8,10},{9,17},{... | collective-permute-start | bytes 1572872 | tf_op jit(solution)/shard_map/ppermute | solution.py:319
  124.7 33.6 %all-to-all-start.2 = ((bf16[8,64,1024]{2,1,0:T(8,128)(2,1)}), bf16[8,64,1024]{2,1,0:T(8,128)(2,1)S(1)}, u32[]{:S(2)}, u32[]{:S(2)}) async-start(bf16[8,64,1024]{2,1,0:T(8,128)(2,1)} %bitcast.8), calls=%async_computation.2 | async-start | bytes 2097152 | tf_op jit(solution)/shard_map/all_to_all | solution.py:245
  134.0 26.3 %copy-start.1 = (bf16[4,64,2048]{2,1,0:T(8,128)(2,1)S(1)}, bf16[4,64,2048]{2,1,0:T(8,128)(2,1)}, u32[]{:S(2)}) copy-start(bf16[4,64,2048]{2,1,0:T(8,128)(2,1)} %get-tuple-element.23) | copy-start | bytes 3145732
  134.0 26.3 %collective-permute-start.4 = (bf16[4,64,2048]{2,1,0:T(8,128)(2,1)}, bf16[4,64,2048]{2,1,0:T(8,128)(2,1)S(1)}, u32[]{:S(2)}, u32[]{:S(2)}) collective-permute-start(bf16[4,64,2048]{2,1,0:T(8,128)(2,1)} %add_dynamic-update-slice_fusion), channel_id=1, source_target_pairs={{0,6},{1,25},{2,0},{3,27},{4,2},{5,29},{6,4},{7,31},{8,14},{9,1},{... | collective-permute-start | bytes 3145736 | tf_op jit(solution)/shard_map/ppermute | solution.py:335
  137.1 23.3 %collective-permute-start.2 = (bf16[4,64,2048]{2,1,0:T(8,128)(2,1)}, bf16[4,64,2048]{2,1,0:T(8,128)(2,1)}, u32[]{:S(2)}, u32[]{:S(2)}) collective-permute-start(bf16[4,64,2048]{2,1,0:T(8,128)(2,1)} %add_dynamic-update-slice_fusion.1), channel_id=1, source_target_pairs={{0,2},{1,9},{2,4},{3,11},{4,6},{5,13},{6,0},{7,15},{8,10},{9,17},{... | collective-permute-start | bytes 3145736 | tf_op jit(solution)/shard_map/ppermute | solution.py:334
  162.1 32.8 %all-to-all-start.3 = ((bf16[8,64,1024]{2,1,0:T(8,128)(2,1)}), bf16[8,64,1024]{2,1,0:T(8,128)(2,1)S(1)}, u32[]{:S(2)}, u32[]{:S(2)}) async-start(bf16[8,64,1024]{2,1,0:T(8,128)(2,1)} %add_rows.1), calls=%async_computation.3 | async-start | bytes 2097152 | tf_op jit(solution)/shard_map/all_to_all | solution.py:245
  165.7 6.4 %collective-permute-start.5 = (bf16[32,2048]{1,0:T(8,128)(2,1)S(1)}, bf16[32,2048]{1,0:T(8,128)(2,1)S(1)}, u32[]{:S(2)}, u32[]{:S(2)}) collective-permute-start(bf16[32,2048]{1,0:T(8,128)(2,1)S(1)} %get-tuple-element.36), channel_id=1, source_target_pairs={{0,8},{1,3},{2,10},{3,5},{4,12},{5,7},{6,14},{7,1},{8,16},{9,11},{... | collective-permute-start | bytes 393224 | tf_op jit(solution)/shard_map/ppermute | solution.py:234
  166.2 6.0 %collective-permute-start.7 = (bf16[32,2048]{1,0:T(8,128)(2,1)S(1)}, bf16[32,2048]{1,0:T(8,128)(2,1)S(1)}, u32[]{:S(2)}, u32[]{:S(2)}) collective-permute-start(bf16[32,2048]{1,0:T(8,128)(2,1)S(1)} %get-tuple-element.37), channel_id=1, source_target_pairs={{0,24},{1,7},{2,26},{3,1},{4,28},{5,3},{6,30},{7,5},{8,0},{9,15},{... | collective-permute-start | bytes 393224 | tf_op jit(solution)/shard_map/ppermute | solution.py:235
  172.2 7.2 %collective-permute-start.8 = (bf16[64,2048]{1,0:T(8,128)(2,1)S(1)}, bf16[64,2048]{1,0:T(8,128)(2,1)S(1)}, u32[]{:S(2)}, u32[]{:S(2)}) collective-permute-start(bf16[64,2048]{1,0:T(8,128)(2,1)S(1)} %get-tuple-element.35), channel_id=1, source_target_pairs={{0,24},{1,7},{2,26},{3,1},{4,28},{5,3},{6,30},{7,5},{8,0},{9,15},{... | collective-permute-start | bytes 786440 | tf_op jit(solution)/shard_map/ppermute | solution.py:239
  175.6 7.6 %collective-permute-start.6 = (bf16[64,2048]{1,0:T(8,128)(2,1)S(1)}, bf16[64,2048]{1,0:T(8,128)(2,1)S(1)}, u32[]{:S(2)}, u32[]{:S(2)}) collective-permute-start(bf16[64,2048]{1,0:T(8,128)(2,1)S(1)} %get-tuple-element.34), channel_id=1, source_target_pairs={{0,8},{1,3},{2,10},{3,5},{4,12},{5,7},{6,14},{7,1},{8,16},{9,11},{... | collective-permute-start | bytes 786440 | tf_op jit(solution)/shard_map/ppermute | solution.py:238
  183.3 1.4 collective-permute-start.9
  210.5 15.6 %all-to-all-start.5 = ((bf16[8,8,2048]{2,1,0:T(8,128)(2,1)}), bf16[8,8,2048]{2,1,0:T(8,128)(2,1)S(1)}, u32[]{:S(2)}, u32[]{:S(2)}) async-start(bf16[8,8,2048]{2,1,0:T(8,128)(2,1)} %broadcast_in_dim.15), calls=%async_computation.5 | async-start | bytes 524288 | tf_op jit(solution)/shard_map/all_to_all | solution.py:245
Sparse Core Ops, SparseCore 0:
  10.6 60.8 all-gather.1

commit v3 on v2

--- a/solution.py
+++ b/solution.py
@@ -40,19 +40,17 @@
     out_ref[...] = total_ref[...].astype(BF16).reshape(out_ref.shape)
 
 
-def pair_kernel(at_ref, own_ref, got_ref, stay_ref, next_ref, prev_ref, up_ref, down_ref):
-    half = up_ref.shape[0]
-
+def pair_kernel(at_ref, own_ref, got_ref, stay_ref, *half_refs):
     def total(d):
         at = lax.rem(at_ref[0] + d, 4)
         return (own_ref[at].astype(F32) + got_ref[at].astype(F32)).astype(BF16)
 
     stay_ref[...] = total(0)
-    next_ref[...] = total(1)
-    prev_ref[...] = total(3)
-    far = total(2)
-    up_ref[...] = far[:half]
-    down_ref[...] = far[half:]
+    for n in range(3):
+        block = total(n + 1)
+        half = block.shape[0] // 2
+        half_refs[2 * n][...] = block[:half]
+        half_refs[2 * n + 1][...] = block[half:]
 
 
 def pair_call(at, own, got):
@@ -66,13 +64,25 @@
     return pl.pallas_call(
         pair_kernel,
         grid=(cols // width,),
-        out_shape=[block_shape] * 3 + [half_shape] * 2,
+        out_shape=[block_shape] + [half_shape] * 6,
         in_specs=[pl.BlockSpec(memory_space=pltpu.SMEM), whole, whole],
-        out_specs=[block] * 3 + [half] * 2,
+        out_specs=[block] + [half] * 6,
         compiler_params=pltpu.CompilerParams(vmem_limit_bytes=58 << 20),
         cost_estimate=pl.CostEstimate(flops=0, bytes_accessed=1 << 10, transcendentals=0),
         name="pair_add",
     )(at, own, got)
+
+
+def ring_kernel(at_ref, stay_ref, low_a_ref, low_b_ref, high_a_ref, high_b_ref, *refs):
+    out_refs, all_ref = refs[:-1], refs[-1]
+    half = low_a_ref.shape[0]
+    for n, (low_ref, high_ref) in enumerate(((low_a_ref, high_a_ref), (low_b_ref, high_b_ref))):
+        mine = stay_ref[pl.ds(n * half, half)].astype(F32)
+        all_ref[pl.ds(n * half, half)] = (
+            mine + low_ref[...].astype(F32) + high_ref[...].astype(F32)
+        ).astype(BF16)
+    for d, out_ref in enumerate(out_refs):
+        out_ref[...] = all_ref[lax.rem(at_ref[0] + d, 4)]
 
 
 def main_kernel(*refs, spans, span_length, chunk):
@@ -226,21 +236,6 @@
     )(core, rows, gain, weight, weight, queries, d_context, *more)
 
 
-def ring_sum(blocks, position, plus, minus):
-    b = [
-        lax.dynamic_index_in_dim(blocks, (position + d) % 4, 0, keepdims=False) for d in range(4)
-    ]
-    half = b[0].shape[0] // 2
-    up = lax.ppermute(b[2][:half], "nbr", plus)
-    down = lax.ppermute(b[2][half:], "nbr", minus)
-    first = lax.dynamic_update_slice(b[1], b[1][:half] + up, (0,) * b[1].ndim)
-    third = lax.dynamic_update_slice(b[3], b[3][half:] + down, (half,) + (0,) * (b[3].ndim - 1))
-    from_low = lax.ppermute(first, "nbr", plus)
-    from_high = lax.ppermute(third, "nbr", minus)
-    total = b[0].astype(F32) + from_low.astype(F32) + from_high.astype(F32)
-    return total.astype(BF16)
-
-
 def swap(array):
     return lax.all_to_all(array, "seq", split_axis=0, concat_axis=0, tiled=True)
 
@@ -314,12 +309,15 @@
     second_at = jnp.where(core == 0, y_at, x_at)
     plus, minus = shifted(0, 1), shifted(0, -1)
     got = lax.ppermute(oth, "nbr", pair)
-    stay, ahead, behind, up, down = pair_call(first_at.reshape(1), own, got)
-    half = up.shape[0]
-    up = lax.ppermute(up, "nbr", plus)
-    down = lax.ppermute(down, "nbr", minus)
-    ahead = lax.dynamic_update_slice(ahead, ahead[:half] + up, (0, 0, 0))
-    behind = lax.dynamic_update_slice(behind, behind[half:] + down, (half, 0, 0))
+    stay, ahead_a, ahead_b, far_a, far_b, behind_a, behind_b = pair_call(
+        first_at.reshape(1), own, got
+    )
+    up = lax.ppermute(far_a, "nbr", plus)
+    down = lax.ppermute(far_b, "nbr", minus)
+    low_b = lax.ppermute(ahead_b, "nbr", plus)
+    high_a = lax.ppermute(behind_a, "nbr", minus)
+    ahead_a = ahead_a + up
+    behind_b = behind_b + down
 
     summed = pl.pallas_call(
         functools.partial(sum_kernel, peers=peers, requests=requests, piece=piece),
@@ -331,12 +329,26 @@
         cost_estimate=pl.CostEstimate(flops=0, bytes_accessed=4 << 20, transcendentals=0),
         name="add_rows",
     )(ids, returned)
-    low = lax.ppermute(ahead, "nbr", plus)
-    high = lax.ppermute(behind, "nbr", minus)
-    part = (stay.astype(F32) + low.astype(F32) + high.astype(F32)).astype(BF16)
-    part, summed = lax.optimization_barrier((part, summed))
+    ahead_a, behind_b, low_b, high_a, summed = lax.optimization_barrier(
+        (ahead_a, behind_b, low_b, high_a, summed)
+    )
     final = swap(summed)
-    part = ring_sum(part, second_at, shifted(1, 1), shifted(1, -1))
+    low_a = lax.ppermute(ahead_a, "nbr", plus)
+    high_b = lax.ppermute(behind_b, "nbr", minus)
+    mine, *others = pl.pallas_call(
+        ring_kernel,
+        out_shape=[jax.ShapeDtypeStruct(stay.shape[1:], BF16)] * 4,
+        in_specs=[smem] + [vmem] * 5,
+        out_specs=[vmem] * 4,
+        scratch_shapes=[pltpu.VMEM(stay.shape, BF16)],
+        compiler_params=pltpu.CompilerParams(vmem_limit_bytes=58 << 20),
+        cost_estimate=pl.CostEstimate(flops=0, bytes_accessed=1 << 10, transcendentals=0),
+        name="ring_add",
+    )(second_at.reshape(1), stay, low_a, low_b, high_a, high_b)
+    part = mine.astype(F32)
+    for d, other in enumerate(others):
+        part = part + lax.ppermute(other, "nbr", shifted(1, d + 1)).astype(F32)
+    part = part.astype(BF16)
 
     part = part.reshape(2, shard_rows, kv_width)
     keep = lax.dynamic_index_in_dim(part, core, 0, keepdims=False)

time: 235 us -> 222 us (0.945)
  waiting for transfers between devices: 92 us -> 73 us
  other arithmetic: 8.05 us -> 3.72 us
  blocking collectives: 54.6 us -> 58.7 us
  Pallas kernels: 35 us -> 38.6 us
    all_to_all x4, waiting for transfers between devices: 68.2 us -> 52.5 us  [swap(): return lax.all_to_all(array, 'seq', split_axis=0, concat_axis=0, tiled=True)]
    dynamic_update_slice x3 -> x0, other arithmetic: 4.18 us -> none  [the longest x1 2.13 us: body(): ahead = lax.dynamic_update_slice(ahead, ahead[:half] + up, (0, 0, 0))]
    all_to_all x2, blocking collectives: 54.6 us -> 58.7 us  [swap(): return lax.all_to_all(array, 'seq', split_axis=0, concat_axis=0, tiled=True)]
    ppermute x1, waiting for transfers between devices: 7.44 us -> 3.84 us  [body(): got = lax.ppermute(oth, 'nbr', pair)]
    pallas_call x0 -> x1, Pallas kernels: none -> 3.59 us  [body(): pl.pallas_call(ring_kernel, out_shape=[jax.ShapeDtypeStruct(stay.shape[1:...]
    ppermute x8 -> x9, starting transfers between devices: 10.9 us -> 12.2 us  [the longest x3 5.83 us: body(): part = part + lax.ppermute(other, 'nbr', shifted(1, d + 1)).astype(F32)]
    ppermute x8 -> x9, waiting for transfers between devices: 14.3 us -> 14.7 us  [the longest x1 7.15 us: body(): low_a = lax.ppermute(ahead_a, 'nbr', plus)]
  transfers between devices with their start and end apart: 15 -> 16, of which waited for: 10 -> 9; matrix products, arithmetic and copies ran while one was open for 4% -> 3% of each run, Pallas kernels for 2% -> 6%
where the time goes in v3:
time: 222 us; the launch traced here: 221 us
  waiting for transfers between devices  73 us (33%)
  blocking collectives  58.7 us (26%)
  Pallas kernels  38.6 us (17%)
  starting transfers between devices  26.6 us (12%)
  between operations  14.3 us (6%)
  local copies, waits for them, and re-layouts  6.34 us (3%)
  other arithmetic  3.72 us (2%)
    all_to_all x2, blocking collectives, swap(): return lax.all_to_all(array, 'seq', split_axis=0, concat_axis=0, tiled=True)  58.7 us
    all_to_all x4, waiting for transfers between devices, swap(): return lax.all_to_all(array, 'seq', split_axis=0, concat_axis=0, tiled=True)  52.5 us
    pallas_call x1, Pallas kernels, attend_call(): pl.pallas_call(functools.partial(main_kernel, spans=spans, span_length=sp...  25.4 us
    all_to_all x4, starting transfers between devices, swap(): return lax.all_to_all(array, 'seq', split_axis=0, concat_axis=0, tiled=True)  14.1 us
    ppermute x1, waiting for transfers between devices, body(): low_a = lax.ppermute(ahead_a, 'nbr', plus)  7.15 us
    ppermute x3, waiting for transfers between devices, body(): part = part + lax.ppermute(other, 'nbr', shifted(1, d + 1)).astype(F32)  6.02 us
    pallas_call x1, Pallas kernels, pair_call(): pl.pallas_call(pair_kernel, grid=(cols // width,), out_shape=[block_shape...  5.9 us
    ppermute x3, starting transfers between devices, body(): part = part + lax.ppermute(other, 'nbr', shifted(1, d + 1)).astype(F32)  5.83 us
  transfers between devices with their start and end apart: 16, of which 9 were waited for; matrix products, arithmetic and copies ran while one was open for 3% of the time, Pallas kernels for 6%

profile of v3, /device:TPU:2, one launch (start us, length us, event | category | flops | bytes accessed | tf_op | source)
XLA Modules:
  0.0 221.2 jit_solution(2157475483705762530)
XLA Ops:
  9.5 39.8 %all_to_all.30.stored_ref = bf16[8,72,1024]{2,1,0:T(8,128)(2,1)S(1)} all-to-all(bf16[8,72,1024]{2,1,0:T(8,128)(2,1)S(1)} %pad_maximum_fusion), channel_id=1, replica_groups=mesh['seq'=8,'nbr'=32] {'seq'}, dimensions={0} | all-to-all | bytes 2359296 | tf_op jit(solution)/shard_map/all_to_all | solution.py:240
  49.4 1.6 pick.1
  51.0 3.6 %all-to-all-start.1 = ((bf16[8,64,1024]{2,1,0:T(8,128)(2,1)}), bf16[8,64,1024]{2,1,0:T(8,128)(2,1)S(1)}, u32[]{:S(2)}, u32[]{:S(2)}) async-start(bf16[8,64,1024]{2,1,0:T(8,128)(2,1)} %pick.1), calls=%async_computation.1 | async-start | bytes 2097152 | tf_op jit(solution)/shard_map/all_to_all | solution.py:240
  54.6 27.5 %all-to-all-done.1 = bf16[8,64,1024]{2,1,0:T(8,128)(2,1)S(1)} async-done(((bf16[8,64,1024]{2,1,0:T(8,128)(2,1)}), bf16[8,64,1024]{2,1,0:T(8,128)(2,1)S(1)}, u32[]{:S(2)}, u32[]{:S(2)}) %all-to-all-start.1) | async-done | bytes 1048608 | tf_op jit(solution)/shard_map/all_to_all | solution.py:240
  83.1 25.4 %attend.1 = (bf16[128,2048]{1,0:T(8,128)(2,1)}, bf16[128,2048]{1,0:T(8,128)(2,1)}, bf16[4,4,64,2048]{3,2,1,0:T(8,128)(2,1)}, bf16[4,4,64,2048]{3,2,1,0:T(8,128)(2,1)}, bf16[8,2,32,1024]{3,2,1,0:T(8,128)(2,1)}) custom-call(s32[1]{0:T(128)} %bitcast.refs_0_, bf16[8,2,32,1024]{3,2,1,0:T(8,128)(2,1)} %bitcast.36, f32[1,1024]{1,0:T(1,128)} %bitcast.37, ...), custom_call_target="tpu_custom_call" | custom-call | flops 14000000000 | bytes 25165824 | tf_op jit(solution)/shard_map/attend/pallas_call | solution.py:198
  108.6 3.6 %all-to-all-start.2 = ((bf16[8,64,1024]{2,1,0:T(8,128)(2,1)}), bf16[8,64,1024]{2,1,0:T(8,128)(2,1)S(1)}, u32[]{:S(2)}, u32[]{:S(2)}) async-start(bf16[8,64,1024]{2,1,0:T(8,128)(2,1)} %bitcast.35), calls=%async_computation.2 | async-start | bytes 2097152 | tf_op jit(solution)/shard_map/all_to_all | solution.py:240
  112.2 3.8 %collective-permute-done.got_ref = bf16[4,4,64,2048]{3,2,1,0:T(8,128)(2,1)} collective-permute-done((bf16[4,4,64,2048]{3,2,1,0:T(8,128)(2,1)}, bf16[4,4,64,2048]{3,2,1,0:T(8,128)(2,1)}, u32[]{:S(2)}, u32[]{:S(2)}) %collective-permute-start) | collective-permute-done | bytes 4194336 | tf_op jit(solution)/shard_map/ppermute | solution.py:311
  116.1 5.9 %pair_add.1 = (bf16[4,64,2048]{2,1,0:T(8,128)(2,1)}, bf16[2,64,2048]{2,1,0:T(8,128)(2,1)}, bf16[2,64,2048]{2,1,0:T(8,128)(2,1)}, bf16[2,64,2048]{2,1,0:T(8,128)(...) custom-call(s32[1]{0:T(128)} %bitcast.8.at_ref, ...), custom_call_target="tpu_custom_call" | custom-call | bytes 1024 | tf_op jit(solution)/shard_map/pair_add/pallas_call | solution.py:64
  122.6 1.5 collective-permute-start.1
  124.1 1.5 collective-permute-start.3
  126.1 15.7 %all-to-all-done.2.grads_ref = bf16[8,64,1024]{2,1,0:T(8,128)(2,1)S(1)} async-done(((bf16[8,64,1024]{2,1,0:T(8,128)(2,1)}), bf16[8,64,1024]{2,1,0:T(8,128)(2,1)S(1)}, u32[]{:S(2)}, u32[]{:S(2)}) %all-to-all-start.2) | async-done | bytes 1048608 | tf_op jit(solution)/shard_map/all_to_all | solution.py:240
  141.8 2.1 add_rows.1
  146.0 3.6 %all-to-all-start.3 = ((bf16[8,64,1024]{2,1,0:T(8,128)(2,1)}), bf16[8,64,1024]{2,1,0:T(8,128)(2,1)S(1)}, u32[]{:S(2)}, u32[]{:S(2)}) async-start(bf16[8,64,1024]{2,1,0:T(8,128)(2,1)} %add_rows.1), calls=%async_computation.3 | async-start | bytes 2097152 | tf_op jit(solution)/shard_map/all_to_all | solution.py:240
  149.6 1.7 collective-permute-start.5
  151.9 7.2 %collective-permute-done.5.low_a_ref = bf16[2,64,2048]{2,1,0:T(8,128)(2,1)S(1)} collective-permute-done((bf16[2,64,2048]{2,1,0:T(8,128)(2,1)S(1)}, bf16[2,64,2048]{2,1,0:T(8,128)(2,1)S(1)}, u32[]{:S(2)}, u32[]{:S(2)}) %collective-permute-start.5) | collective-permute-done | bytes 524320 | tf_op jit(solution)/shard_map/ppermute | solution.py:336
  159.0 1.5 collective-permute-done.6.high_b_ref
  161.3 3.6 %ring_add.1 = (bf16[64,2048]{1,0:T(8,128)(2,1)}, bf16[64,2048]{1,0:T(8,128)(2,1)}, bf16[64,2048]{1,0:T(8,128)(2,1)}, bf16[64,2048]{1,0:T(8,128)(2,1)}) custom-call(s32[1]{0:T(128)} %bitcast.7.at_ref, bf16[4,64,2048]{2,1,0:T(8,128)(2,1)} %get-tuple-element.32.stay_ref, bf16[2,64,2048]{2,1,0:T(8,128)(2,1)} %copy-done.4, ...), custom_call_target="tpu_custom_call" | custom-call | bytes 1024 | tf_op jit(solution)/shard_map/ring_add/pallas_call | solution.py:338
  164.9 1.6 collective-permute-start.7
  166.5 2.9 %collective-permute-start.8 = (bf16[64,2048]{1,0:T(8,128)(2,1)}, bf16[64,2048]{1,0:T(8,128)(2,1)S(1)}, u32[]{:S(2)}, u32[]{:S(2)}) collective-permute-start(bf16[64,2048]{1,0:T(8,128)(2,1)} %get-tuple-element.46), channel_id=1, source_target_pairs={{0,16},{1,5},{2,18},{3,7},{4,20},{5,1},{6,22},{7,3},{8,24},{9,13},... | collective-permute-start | bytes 786440 | tf_op jit(solution)/shard_map/ppermute | solution.py:350
  170.7 2.0 collective-permute-done.7
  172.7 4.0 %collective-permute-done.8 = bf16[64,2048]{1,0:T(8,128)(2,1)S(1)} collective-permute-done((bf16[64,2048]{1,0:T(8,128)(2,1)}, bf16[64,2048]{1,0:T(8,128)(2,1)S(1)}, u32[]{:S(2)}, u32[]{:S(2)}) %collective-permute-start.8) | collective-permute-done | bytes 262176 | tf_op jit(solution)/shard_map/ppermute | solution.py:350
  179.4 18.9 %all_to_all.31 = bf16[8,8,2048]{2,1,0:T(8,128)(2,1)S(1)} all-to-all(bf16[8,8,2048]{2,1,0:T(8,128)(2,1)S(1)} %pad_maximum_fusion.2), channel_id=1, replica_groups=mesh['seq'=8,'nbr'=32] {'seq'}, dimensions={0} | all-to-all | bytes 524288 | tf_op jit(solution)/shard_map/all_to_all | solution.py:240
  199.0 3.4 %all-to-all-start.5 = ((bf16[8,8,2048]{2,1,0:T(8,128)(2,1)}), bf16[8,8,2048]{2,1,0:T(8,128)(2,1)S(1)}, u32[]{:S(2)}, u32[]{:S(2)}) async-start(bf16[8,8,2048]{2,1,0:T(8,128)(2,1)} %broadcast_in_dim.15), calls=%async_computation.5 | async-start | bytes 524288 | tf_op jit(solution)/shard_map/all_to_all | solution.py:240
  204.1 9.3 %all-to-all-done.5 = bf16[8,8,2048]{2,1,0:T(8,128)(2,1)S(1)} async-done(((bf16[8,8,2048]{2,1,0:T(8,128)(2,1)}), bf16[8,8,2048]{2,1,0:T(8,128)(2,1)S(1)}, u32[]{:S(2)}, u32[]{:S(2)}) %all-to-all-start.5) | async-done | bytes 262176 | tf_op jit(solution)/shard_map/all_to_all | solution.py:240
  (53 shorter events, 15.4 us)
Async XLA Ops:
  7.2 2.1 copy-start.7
  7.2 2.1 copy-start.6
  7.2 74.9 %all-gather.2.cloned.1.call-start = ((), (), s32[]{:S(2)}) async-start(), calls=%async_computation.6 | async-start | bytes 8650752 | tf_op jit(solution)/shard_map/all_gather | solution.py:257
  51.0 31.1 %all-to-all-start.1 = ((bf16[8,64,1024]{2,1,0:T(8,128)(2,1)}), bf16[8,64,1024]{2,1,0:T(8,128)(2,1)S(1)}, u32[]{:S(2)}, u32[]{:S(2)}) async-start(bf16[8,64,1024]{2,1,0:T(8,128)(2,1)} %pick.1), calls=%async_computation.1 | async-start | bytes 2097152 | tf_op jit(solution)/shard_map/all_to_all | solution.py:240
  82.1 1.0 copy-start
  108.5 7.6 %collective-permute-start = (bf16[4,4,64,2048]{3,2,1,0:T(8,128)(2,1)}, bf16[4,4,64,2048]{3,2,1,0:T(8,128)(2,1)}, u32[]{:S(2)}, u32[]{:S(2)}) collective-permute-start(bf16[4,4,64,2048]{3,2,1,0:T(8,128)(2,1)} %get-tuple-element.31), channel_id=1, source_target_pairs={{0,1},{1,0},{2,3},{3,2},{4,5},{5,4},{6,7},{7,6},{8,9},{9,8},{10,11... | collective-permute-start | bytes 12582920 | tf_op jit(solution)/shard_map/ppermute | solution.py:311
  108.6 33.2 %all-to-all-start.2 = ((bf16[8,64,1024]{2,1,0:T(8,128)(2,1)}), bf16[8,64,1024]{2,1,0:T(8,128)(2,1)S(1)}, u32[]{:S(2)}, u32[]{:S(2)}) async-start(bf16[8,64,1024]{2,1,0:T(8,128)(2,1)} %bitcast.35), calls=%async_computation.2 | async-start | bytes 2097152 | tf_op jit(solution)/shard_map/all_to_all | solution.py:240
  122.0 22.7 %copy-start.2 = (bf16[2,64,2048]{2,1,0:T(8,128)(2,1)S(1)}, bf16[2,64,2048]{2,1,0:T(8,128)(2,1)}, u32[]{:S(2)}) copy-start(bf16[2,64,2048]{2,1,0:T(8,128)(2,1)} %get-tuple-element.35) | copy-start | bytes 1572868
  122.0 23.9 %copy-start.1 = (bf16[2,64,2048]{2,1,0:T(8,128)(2,1)S(1)}, bf16[2,64,2048]{2,1,0:T(8,128)(2,1)}, u32[]{:S(2)}) copy-start(bf16[2,64,2048]{2,1,0:T(8,128)(2,1)} %get-tuple-element.33) | copy-start | bytes 1572868
  122.0 21.9 %collective-permute-start.2 = (bf16[2,64,2048]{2,1,0:T(8,128)(2,1)}, bf16[2,64,2048]{2,1,0:T(8,128)(2,1)S(1)}, u32[]{:S(2)}, u32[]{:S(2)}) collective-permute-start(bf16[2,64,2048]{2,1,0:T(8,128)(2,1)} %get-tuple-element.36), channel_id=1, source_target_pairs={{0,6},{1,25},{2,0},{3,27},{4,2},{5,29},{6,4},{7,31},{8,14},{9,1},{... | collective-permute-start | bytes 1572872 | tf_op jit(solution)/shard_map/ppermute | solution.py:316
  122.6 23.2 %collective-permute-start.1 = (bf16[2,64,2048]{2,1,0:T(8,128)(2,1)}, bf16[2,64,2048]{2,1,0:T(8,128)(2,1)S(1)}, u32[]{:S(2)}, u32[]{:S(2)}) collective-permute-start(bf16[2,64,2048]{2,1,0:T(8,128)(2,1)} %get-tuple-element.34), channel_id=1, source_target_pairs={{0,2},{1,9},{2,4},{3,11},{4,6},{5,13},{6,0},{7,15},{8,10},{9,17},{... | collective-permute-start | bytes 1572872 | tf_op jit(solution)/shard_map/ppermute | solution.py:315
  124.1 21.9 %collective-permute-start.3 = (bf16[2,64,2048]{2,1,0:T(8,128)(2,1)}, bf16[2,64,2048]{2,1,0:T(8,128)(2,1)}, u32[]{:S(2)}, u32[]{:S(2)}) collective-permute-start(bf16[2,64,2048]{2,1,0:T(8,128)(2,1)} %get-tuple-element.37), channel_id=1, source_target_pairs={{0,2},{1,9},{2,4},{3,11},{4,6},{5,13},{6,0},{7,15},{8,10},{9,17},{... | collective-permute-start | bytes 1572872 | tf_op jit(solution)/shard_map/ppermute | solution.py:317
  125.6 20.4 %collective-permute-start.4 = (bf16[2,64,2048]{2,1,0:T(8,128)(2,1)}, bf16[2,64,2048]{2,1,0:T(8,128)(2,1)}, u32[]{:S(2)}, u32[]{:S(2)}) collective-permute-start(bf16[2,64,2048]{2,1,0:T(8,128)(2,1)} %get-tuple-element.38), channel_id=1, source_target_pairs={{0,6},{1,25},{2,0},{3,27},{4,2},{5,29},{6,4},{7,31},{8,14},{9,1},{... | collective-permute-start | bytes 1572872 | tf_op jit(solution)/shard_map/ppermute | solution.py:318
  143.8 0.8 copy-start.3
  146.0 33.3 %all-to-all-start.3 = ((bf16[8,64,1024]{2,1,0:T(8,128)(2,1)}), bf16[8,64,1024]{2,1,0:T(8,128)(2,1)S(1)}, u32[]{:S(2)}, u32[]{:S(2)}) async-start(bf16[8,64,1024]{2,1,0:T(8,128)(2,1)} %add_rows.1), calls=%async_computation.3 | async-start | bytes 2097152 | tf_op jit(solution)/shard_map/all_to_all | solution.py:240
  149.6 9.4 %collective-permute-start.5 = (bf16[2,64,2048]{2,1,0:T(8,128)(2,1)S(1)}, bf16[2,64,2048]{2,1,0:T(8,128)(2,1)S(1)}, u32[]{:S(2)}, u32[]{:S(2)}) collective-permute-start(bf16[2,64,2048]{2,1,0:T(8,128)(2,1)S(1)} %add.40), channel_id=1, source_target_pairs={{0,2},{1,9},{2,4},{3,11},{4,6},{5,13},{6,0},{7,15},{8,10},{9,17},{... | collective-permute-start | bytes 1572872 | tf_op jit(solution)/shard_map/ppermute | solution.py:336
  151.3 9.2 %collective-permute-start.6 = (bf16[2,64,2048]{2,1,0:T(8,128)(2,1)S(1)}, bf16[2,64,2048]{2,1,0:T(8,128)(2,1)S(1)}, u32[]{:S(2)}, u32[]{:S(2)}) collective-permute-start(bf16[2,64,2048]{2,1,0:T(8,128)(2,1)S(1)} %add.41), channel_id=1, source_target_pairs={{0,6},{1,25},{2,0},{3,27},{4,2},{5,29},{6,4},{7,31},{8,14},{9,1},{... | collective-permute-start | bytes 1572872 | tf_op jit(solution)/shard_map/ppermute | solution.py:337
  159.0 1.5 copy-start.4
  160.5 0.8 copy-start.5
  164.9 7.8 %collective-permute-start.7 = (bf16[64,2048]{1,0:T(8,128)(2,1)}, bf16[64,2048]{1,0:T(8,128)(2,1)S(1)}, u32[]{:S(2)}, u32[]{:S(2)}) collective-permute-start(bf16[64,2048]{1,0:T(8,128)(2,1)} %get-tuple-element.45), channel_id=1, source_target_pairs={{0,8},{1,3},{2,10},{3,5},{4,12},{5,7},{6,14},{7,1},{8,16},{9,11},{... | collective-permute-start | bytes 786440 | tf_op jit(solution)/shard_map/ppermute | solution.py:350
  166.5 10.3 %collective-permute-start.8 = (bf16[64,2048]{1,0:T(8,128)(2,1)}, bf16[64,2048]{1,0:T(8,128)(2,1)S(1)}, u32[]{:S(2)}, u32[]{:S(2)}) collective-permute-start(bf16[64,2048]{1,0:T(8,128)(2,1)} %get-tuple-element.46), channel_id=1, source_target_pairs={{0,16},{1,5},{2,18},{3,7},{4,20},{5,1},{6,22},{7,3},{8,24},{9,13},... | collective-permute-start | bytes 786440 | tf_op jit(solution)/shard_map/ppermute | solution.py:350
  169.4 7.4 %collective-permute-start.9 = (bf16[64,2048]{1,0:T(8,128)(2,1)}, bf16[64,2048]{1,0:T(8,128)(2,1)S(1)}, u32[]{:S(2)}, u32[]{:S(2)}) collective-permute-start(bf16[64,2048]{1,0:T(8,128)(2,1)} %get-tuple-element.47), channel_id=1, source_target_pairs={{0,24},{1,7},{2,26},{3,1},{4,28},{5,3},{6,30},{7,5},{8,0},{9,15},{... | collective-permute-start | bytes 786440 | tf_op jit(solution)/shard_map/ppermute | solution.py:350
  177.9 1.4 collective-permute-start.10
  199.0 14.5 %all-to-all-start.5 = ((bf16[8,8,2048]{2,1,0:T(8,128)(2,1)}), bf16[8,8,2048]{2,1,0:T(8,128)(2,1)S(1)}, u32[]{:S(2)}, u32[]{:S(2)}) async-start(bf16[8,8,2048]{2,1,0:T(8,128)(2,1)} %broadcast_in_dim.15), calls=%async_computation.5 | async-start | bytes 524288 | tf_op jit(solution)/shard_map/all_to_all | solution.py:240
Sparse Core Ops, SparseCore 0:
  10.6 60.8 all-gather.1

commit v4 on v3

--- a/solution.py
+++ b/solution.py
@@ -55,7 +55,7 @@
 
 def pair_call(at, own, got):
     ring, chips, rows, cols = own.shape
-    width = 512
+    width = 1024
     whole = pl.BlockSpec((ring, chips, rows, width), lambda i: (0, 0, 0, i))
     block = pl.BlockSpec((chips, rows, width), lambda i: (0, 0, i))
     half = pl.BlockSpec((chips // 2, rows, width), lambda i: (0, 0, i))
@@ -71,6 +71,11 @@
         cost_estimate=pl.CostEstimate(flops=0, bytes_accessed=1 << 10, transcendentals=0),
         name="pair_add",
     )(at, own, got)
+
+
+def add_kernel(a_ref, b_ref, c_ref, d_ref, first_ref, second_ref):
+    first_ref[...] = (a_ref[...].astype(F32) + b_ref[...].astype(F32)).astype(BF16)
+    second_ref[...] = (c_ref[...].astype(F32) + d_ref[...].astype(F32)).astype(BF16)
 
 
 def ring_kernel(at_ref, stay_ref, low_a_ref, low_b_ref, high_a_ref, high_b_ref, *refs):
@@ -226,7 +231,7 @@
             pltpu.VMEM((tokens, step_cols), BF16),
         ],
         input_output_aliases={8: 0, 9: 1} if more else {},
-        compiler_params=pltpu.CompilerParams(vmem_limit_bytes=58 << 20),
+        compiler_params=pltpu.CompilerParams(vmem_limit_bytes=50 << 20),
         cost_estimate=pl.CostEstimate(
             flops=14_000_000_000 // CHUNKS,
             bytes_accessed=24 << 20,
@@ -316,8 +321,15 @@
     down = lax.ppermute(far_b, "nbr", minus)
     low_b = lax.ppermute(ahead_b, "nbr", plus)
     high_a = lax.ppermute(behind_a, "nbr", minus)
-    ahead_a = ahead_a + up
-    behind_b = behind_b + down
+    ahead_a, behind_b = pl.pallas_call(
+        add_kernel,
+        out_shape=[jax.ShapeDtypeStruct(up.shape, BF16)] * 2,
+        in_specs=[vmem] * 4,
+        out_specs=[vmem] * 2,
+        compiler_params=pltpu.CompilerParams(vmem_limit_bytes=58 << 20),
+        cost_estimate=pl.CostEstimate(flops=0, bytes_accessed=1 << 10, transcendentals=0),
+        name="add_two",
+    )(ahead_a, up, behind_b, down)
 
     summed = pl.pallas_call(
         functools.partial(sum_kernel, peers=peers, requests=requests, piece=piece),
@@ -329,12 +341,12 @@
         cost_estimate=pl.CostEstimate(flops=0, bytes_accessed=4 << 20, transcendentals=0),
         name="add_rows",
     )(ids, returned)
-    ahead_a, behind_b, low_b, high_a, summed = lax.optimization_barrier(
-        (ahead_a, behind_b, low_b, high_a, summed)
+    low_a = lax.ppermute(ahead_a, "nbr", plus)
+    high_b = lax.ppermute(behind_b, "nbr", minus)
+    low_a, low_b, high_a, high_b, summed = lax.optimization_barrier(
+        (low_a, low_b, high_a, high_b, summed)
     )
     final = swap(summed)
-    low_a = lax.ppermute(ahead_a, "nbr", plus)
-    high_b = lax.ppermute(behind_b, "nbr", minus)
     mine, *others = pl.pallas_call(
         ring_kernel,
         out_shape=[jax.ShapeDtypeStruct(stay.shape[1:], BF16)] * 4,

time: 222 us -> 215 us (0.968)
  blocking collectives: 58.7 us -> 54.5 us
    ppermute x1, waiting for transfers between devices: 7.15 us -> 1.11 us  [body(): low_a = lax.ppermute(ahead_a, 'nbr', plus)]
    ppermute x1, waiting for transfers between devices: 0.01 us -> 5.34 us  [body(): up = lax.ppermute(far_a, 'nbr', plus)]
    all_to_all x2, blocking collectives: 58.7 us -> 54.5 us  [swap(): return lax.all_to_all(array, 'seq', split_axis=0, concat_axis=0, tiled=True)]
    pallas_call x0 -> x1, Pallas kernels: none -> 2.6 us  [body(): pl.pallas_call(add_kernel, out_shape=[jax.ShapeDtypeStruct(up.shape, BF16...]
  transfers between devices with their start and end apart: 16 -> 16, of which waited for: 9 -> 12; matrix products, arithmetic and copies ran while one was open for 3% -> 2% of each run, Pallas kernels for 6% -> 7%
where the time goes in v4:
time: 215 us; the launch traced here: 214 us
  waiting for transfers between devices  72.4 us (34%)
  blocking collectives  54.5 us (25%)
  Pallas kernels  39.8 us (19%)
  starting transfers between devices  26.3 us (12%)
  between operations  14.3 us (7%)
  local copies, waits for them, and re-layouts  4.56 us (2%)
  other arithmetic  2.42 us (1%)
    all_to_all x2, blocking collectives, swap(): return lax.all_to_all(array, 'seq', split_axis=0, concat_axis=0, tiled=True)  54.5 us
    all_to_all x4, waiting for transfers between devices, swap(): return lax.all_to_all(array, 'seq', split_axis=0, concat_axis=0, tiled=True)  51.4 us
    pallas_call x1, Pallas kernels, attend_call(): pl.pallas_call(functools.partial(main_kernel, spans=spans, span_length=sp...  24.7 us
    all_to_all x4, starting transfers between devices, swap(): return lax.all_to_all(array, 'seq', split_axis=0, concat_axis=0, tiled=True)  14.1 us
    ppermute x3, waiting for transfers between devices, body(): part = part + lax.ppermute(other, 'nbr', shifted(1, d + 1)).astype(F32)  6.02 us
    ppermute x3, starting transfers between devices, body(): part = part + lax.ppermute(other, 'nbr', shifted(1, d + 1)).astype(F32)  5.83 us
    ppermute x1, waiting for transfers between devices, body(): up = lax.ppermute(far_a, 'nbr', plus)  5.34 us
    pallas_call x1, Pallas kernels, pair_call(): pl.pallas_call(pair_kernel, grid=(cols // width,), out_shape=[block_shape...  5.2 us
  transfers between devices with their start and end apart: 16, of which 12 were waited for; matrix products, arithmetic and copies ran while one was open for 2% of the time, Pallas kernels for 7%

profile of v4, /device:TPU:2, one launch (start us, length us, event | category | flops | bytes accessed | tf_op | source)
XLA Modules:
  0.0 214.3 jit_solution(12156010675123582633)
XLA Ops:
  9.5 39.8 %all_to_all.30.stored_ref = bf16[8,72,1024]{2,1,0:T(8,128)(2,1)S(1)} all-to-all(bf16[8,72,1024]{2,1,0:T(8,128)(2,1)S(1)} %pad_maximum_fusion), channel_id=1, replica_groups=mesh['seq'=8,'nbr'=32] {'seq'}, dimensions={0} | all-to-all | bytes 2359296 | tf_op jit(solution)/shard_map/all_to_all | solution.py:245
  49.4 1.6 pick.1
  51.0 3.6 %all-to-all-start.1 = ((bf16[8,64,1024]{2,1,0:T(8,128)(2,1)}), bf16[8,64,1024]{2,1,0:T(8,128)(2,1)S(1)}, u32[]{:S(2)}, u32[]{:S(2)}) async-start(bf16[8,64,1024]{2,1,0:T(8,128)(2,1)} %pick.1), calls=%async_computation.1 | async-start | bytes 2097152 | tf_op jit(solution)/shard_map/all_to_all | solution.py:245
  54.6 27.5 %all-to-all-done.1 = bf16[8,64,1024]{2,1,0:T(8,128)(2,1)S(1)} async-done(((bf16[8,64,1024]{2,1,0:T(8,128)(2,1)}), bf16[8,64,1024]{2,1,0:T(8,128)(2,1)S(1)}, u32[]{:S(2)}, u32[]{:S(2)}) %all-to-all-start.1) | async-done | bytes 1048608 | tf_op jit(solution)/shard_map/all_to_all | solution.py:245
  82.1 24.7 %attend.1 = (bf16[128,2048]{1,0:T(8,128)(2,1)}, bf16[128,2048]{1,0:T(8,128)(2,1)}, bf16[4,4,64,2048]{3,2,1,0:T(8,128)(2,1)}, bf16[4,4,64,2048]{3,2,1,0:T(8,128)(2,1)}, bf16[8,2,32,1024]{3,2,1,0:T(8,128)(2,1)}) custom-call(s32[1]{0:T(128)} %bitcast.refs_0_, bf16[8,2,32,1024]{3,2,1,0:T(8,128)(2,1)S(1)} %bitcast.30, f32[1,1024]{1,0:T(1,128)S(1)} %bitcast.31, ...), custom_call_target="tpu_custom_call" | custom-call | flops 14000000000 | bytes 25165824 | tf_op jit(solution)/shard_map/attend/pallas_call | solution.py:203
  106.9 3.6 %all-to-all-start.2 = ((bf16[8,64,1024]{2,1,0:T(8,128)(2,1)}), bf16[8,64,1024]{2,1,0:T(8,128)(2,1)S(1)}, u32[]{:S(2)}, u32[]{:S(2)}) async-start(bf16[8,64,1024]{2,1,0:T(8,128)(2,1)} %bitcast.9), calls=%async_computation.2 | async-start | bytes 2097152 | tf_op jit(solution)/shard_map/all_to_all | solution.py:245
  110.6 3.8 %collective-permute-done.got_ref = bf16[4,4,64,2048]{3,2,1,0:T(8,128)(2,1)} collective-permute-done((bf16[4,4,64,2048]{3,2,1,0:T(8,128)(2,1)}, bf16[4,4,64,2048]{3,2,1,0:T(8,128)(2,1)}, u32[]{:S(2)}, u32[]{:S(2)}) %collective-permute-start) | collective-permute-done | bytes 4194336 | tf_op jit(solution)/shard_map/ppermute | solution.py:316
  114.4 5.2 %pair_add.1 = (bf16[4,64,2048]{2,1,0:T(8,128)(2,1)}, bf16[2,64,2048]{2,1,0:T(8,128)(2,1)}, bf16[2,64,2048]{2,1,0:T(8,128)(2,1)}, bf16[2,64,2048]{2,1,0:T(8,128)(...) custom-call(s32[1]{0:T(128)} %bitcast.8.at_ref, ...), custom_call_target="tpu_custom_call" | custom-call | bytes 1024 | tf_op jit(solution)/shard_map/pair_add/pallas_call | solution.py:64
  119.6 1.5 collective-permute-start.1
  121.6 1.5 collective-permute-start.4
  123.7 5.3 %collective-permute-done.1.b_ref = bf16[2,64,2048]{2,1,0:T(8,128)(2,1)S(1)} collective-permute-done((bf16[2,64,2048]{2,1,0:T(8,128)(2,1)}, bf16[2,64,2048]{2,1,0:T(8,128)(2,1)S(1)}, u32[]{:S(2)}, u32[]{:S(2)}) %collective-permute-start.1) | collective-permute-done | bytes 524320 | tf_op jit(solution)/shard_map/ppermute | solution.py:320
  131.3 2.6 %add_two.1 = (bf16[2,64,2048]{2,1,0:T(8,128)(2,1)}, bf16[2,64,2048]{2,1,0:T(8,128)(2,1)}) custom-call(bf16[2,64,2048]{2,1,0:T(8,128)(2,1)} %get-tuple-element.35.a_ref, bf16[2,64,2048]{2,1,0:T(8,128)(2,1)} %copy-done.7, bf16[2,64,2048]{2,1,0:T(8,128)(2,1)} %get-tuple-element.37.c_ref, bf16[2,64,2048]{2,1,0:T(8,128)(2,1)} %copy-done.8), custom_call_target="tpu_custom_call" | custom-call | bytes 1024 | tf_op jit(solution)/shard_map/add_two/pallas_call | solution.py:324
  135.9 4.2 %all-to-all-done.2.grads_ref = bf16[8,64,1024]{2,1,0:T(8,128)(2,1)S(1)} async-done(((bf16[8,64,1024]{2,1,0:T(8,128)(2,1)}), bf16[8,64,1024]{2,1,0:T(8,128)(2,1)S(1)}, u32[]{:S(2)}, u32[]{:S(2)}) %all-to-all-start.2) | async-done | bytes 1048608 | tf_op jit(solution)/shard_map/all_to_all | solution.py:245
  140.1 2.0 add_rows.1
  144.5 3.6 %all-to-all-start.3 = ((bf16[8,64,1024]{2,1,0:T(8,128)(2,1)}), bf16[8,64,1024]{2,1,0:T(8,128)(2,1)S(1)}, u32[]{:S(2)}, u32[]{:S(2)}) async-start(bf16[8,64,1024]{2,1,0:T(8,128)(2,1)} %add_rows.1), calls=%async_computation.3 | async-start | bytes 2097152 | tf_op jit(solution)/shard_map/all_to_all | solution.py:245
  148.1 3.6 %ring_add.1 = (bf16[64,2048]{1,0:T(8,128)(2,1)}, bf16[64,2048]{1,0:T(8,128)(2,1)}, bf16[64,2048]{1,0:T(8,128)(2,1)}, bf16[64,2048]{1,0:T(8,128)(2,1)}) custom-call(s32[1]{0:T(128)} %bitcast.7.at_ref, bf16[4,64,2048]{2,1,0:T(8,128)(2,1)} %get-tuple-element.34.stay_ref, bf16[2,64,2048]{2,1,0:T(8,128)(2,1)} %copy-done.5, bf16[2,64,2048]{2,1,0:T(8,128)(2,1)} %copy-done.3, ...), custom_call_target="tpu_custom_call" | custom-call | bytes 1024 | tf_op jit(solution)/shard_map/ring_add/pallas_call | solution.py:350
  151.7 1.6 collective-permute-start.7
  153.2 2.9 %collective-permute-start.8 = (bf16[64,2048]{1,0:T(8,128)(2,1)}, bf16[64,2048]{1,0:T(8,128)(2,1)S(1)}, u32[]{:S(2)}, u32[]{:S(2)}) collective-permute-start(bf16[64,2048]{1,0:T(8,128)(2,1)} %get-tuple-element.50), channel_id=1, source_target_pairs={{0,16},{1,5},{2,18},{3,7},{4,20},{5,1},{6,22},{7,3},{8,24},{9,13},... | collective-permute-start | bytes 786440 | tf_op jit(solution)/shard_map/ppermute | solution.py:362
  157.5 2.0 collective-permute-done.7
  159.5 4.0 %collective-permute-done.8 = bf16[64,2048]{1,0:T(8,128)(2,1)S(1)} collective-permute-done((bf16[64,2048]{1,0:T(8,128)(2,1)}, bf16[64,2048]{1,0:T(8,128)(2,1)S(1)}, u32[]{:S(2)}, u32[]{:S(2)}) %collective-permute-start.8) | collective-permute-done | bytes 262176 | tf_op jit(solution)/shard_map/ppermute | solution.py:362
  166.1 9.4 %all-to-all-done.3 = bf16[8,64,1024]{2,1,0:T(8,128)(2,1)S(1)} async-done(((bf16[8,64,1024]{2,1,0:T(8,128)(2,1)}), bf16[8,64,1024]{2,1,0:T(8,128)(2,1)S(1)}, u32[]{:S(2)}, u32[]{:S(2)}) %all-to-all-start.3) | async-done | bytes 1048608 | tf_op jit(solution)/shard_map/all_to_all | solution.py:245
  175.5 14.7 %all_to_all.31 = bf16[8,8,2048]{2,1,0:T(8,128)(2,1)S(1)} all-to-all(bf16[8,8,2048]{2,1,0:T(8,128)(2,1)S(1)} %pad_maximum_fusion.2), channel_id=1, replica_groups=mesh['seq'=8,'nbr'=32] {'seq'}, dimensions={0} | all-to-all | bytes 524288 | tf_op jit(solution)/shard_map/all_to_all | solution.py:245
  191.0 3.4 %all-to-all-start.5 = ((bf16[8,8,2048]{2,1,0:T(8,128)(2,1)}), bf16[8,8,2048]{2,1,0:T(8,128)(2,1)S(1)}, u32[]{:S(2)}, u32[]{:S(2)}) async-start(bf16[8,8,2048]{2,1,0:T(8,128)(2,1)} %broadcast_in_dim.15), calls=%async_computation.5 | async-start | bytes 524288 | tf_op jit(solution)/shard_map/all_to_all | solution.py:245
  196.2 10.4 %all-to-all-done.5 = bf16[8,8,2048]{2,1,0:T(8,128)(2,1)S(1)} async-done(((bf16[8,8,2048]{2,1,0:T(8,128)(2,1)}), bf16[8,8,2048]{2,1,0:T(8,128)(2,1)S(1)}, u32[]{:S(2)}, u32[]{:S(2)}) %all-to-all-start.5) | async-done | bytes 262176 | tf_op jit(solution)/shard_map/all_to_all | solution.py:245
  (58 shorter events, 17.5 us)
Async XLA Ops:
  7.2 2.1 copy-start.10
  7.2 74.9 %all-gather.2.cloned.1.call-start = ((), (), s32[]{:S(2)}) async-start(), calls=%async_computation.6 | async-start | bytes 8650752 | tf_op jit(solution)/shard_map/all_gather | solution.py:262
  49.4 32.7 %copy-start = (bf16[128,2048]{1,0:T(8,128)(2,1)S(1)}, bf16[128,2048]{1,0:T(8,128)(2,1)}, u32[]{:S(2)}) copy-start(bf16[128,2048]{1,0:T(8,128)(2,1)} %refs_5_.1) | copy-start | bytes 1572868
  49.4 32.7 %copy-start.1 = (bf16[128,2048]{1,0:T(8,128)(2,1)S(1)}, bf16[128,2048]{1,0:T(8,128)(2,1)}, u32[]{:S(2)}) copy-start(bf16[128,2048]{1,0:T(8,128)(2,1)} %refs_6_.1) | copy-start | bytes 1572868
  49.4 32.7 %copy-start.2 = (f32[1024]{0:T(1024)S(1)}, f32[1024]{0:T(1024)}, u32[]{:S(2)}) copy-start(f32[1024]{0:T(1024)} %param.12) | copy-start | bytes 12292
  51.0 31.1 %all-to-all-start.1 = ((bf16[8,64,1024]{2,1,0:T(8,128)(2,1)}), bf16[8,64,1024]{2,1,0:T(8,128)(2,1)S(1)}, u32[]{:S(2)}, u32[]{:S(2)}) async-start(bf16[8,64,1024]{2,1,0:T(8,128)(2,1)} %pick.1), calls=%async_computation.1 | async-start | bytes 2097152 | tf_op jit(solution)/shard_map/all_to_all | solution.py:245
  106.8 7.6 %collective-permute-start = (bf16[4,4,64,2048]{3,2,1,0:T(8,128)(2,1)}, bf16[4,4,64,2048]{3,2,1,0:T(8,128)(2,1)}, u32[]{:S(2)}, u32[]{:S(2)}) collective-permute-start(bf16[4,4,64,2048]{3,2,1,0:T(8,128)(2,1)} %get-tuple-element.33), channel_id=1, source_target_pairs={{0,1},{1,0},{2,3},{3,2},{4,5},{5,4},{6,7},{7,6},{8,9},{9,8},{10,11... | collective-permute-start | bytes 12582920 | tf_op jit(solution)/shard_map/ppermute | solution.py:316
  106.9 33.2 %all-to-all-start.2 = ((bf16[8,64,1024]{2,1,0:T(8,128)(2,1)}), bf16[8,64,1024]{2,1,0:T(8,128)(2,1)S(1)}, u32[]{:S(2)}, u32[]{:S(2)}) async-start(bf16[8,64,1024]{2,1,0:T(8,128)(2,1)} %bitcast.9), calls=%async_computation.2 | async-start | bytes 2097152 | tf_op jit(solution)/shard_map/all_to_all | solution.py:245
  119.6 9.4 %collective-permute-start.1 = (bf16[2,64,2048]{2,1,0:T(8,128)(2,1)}, bf16[2,64,2048]{2,1,0:T(8,128)(2,1)S(1)}, u32[]{:S(2)}, u32[]{:S(2)}) collective-permute-start(bf16[2,64,2048]{2,1,0:T(8,128)(2,1)} %get-tuple-element.36), channel_id=1, source_target_pairs={{0,2},{1,9},{2,4},{3,11},{4,6},{5,13},{6,0},{7,15},{8,10},{9,17},{... | collective-permute-start | bytes 1572872 | tf_op jit(solution)/shard_map/ppermute | solution.py:320
  121.1 9.4 %collective-permute-start.2 = (bf16[2,64,2048]{2,1,0:T(8,128)(2,1)}, bf16[2,64,2048]{2,1,0:T(8,128)(2,1)S(1)}, u32[]{:S(2)}, u32[]{:S(2)}) collective-permute-start(bf16[2,64,2048]{2,1,0:T(8,128)(2,1)} %get-tuple-element.38), channel_id=1, source_target_pairs={{0,6},{1,25},{2,0},{3,27},{4,2},{5,29},{6,4},{7,31},{8,14},{9,1},{... | collective-permute-start | bytes 1572872 | tf_op jit(solution)/shard_map/ppermute | solution.py:321
  121.6 20.5 %collective-permute-start.4 = (bf16[2,64,2048]{2,1,0:T(8,128)(2,1)}, bf16[2,64,2048]{2,1,0:T(8,128)(2,1)S(1)}, u32[]{:S(2)}, u32[]{:S(2)}) collective-permute-start(bf16[2,64,2048]{2,1,0:T(8,128)(2,1)} %get-tuple-element.40), channel_id=1, source_target_pairs={{0,2},{1,9},{2,4},{3,11},{4,6},{5,13},{6,0},{7,15},{8,10},{9,17},{... | collective-permute-start | bytes 1572872 | tf_op jit(solution)/shard_map/ppermute | solution.py:322
  123.1 19.0 %collective-permute-start.5 = (bf16[2,64,2048]{2,1,0:T(8,128)(2,1)}, bf16[2,64,2048]{2,1,0:T(8,128)(2,1)S(1)}, u32[]{:S(2)}, u32[]{:S(2)}) collective-permute-start(bf16[2,64,2048]{2,1,0:T(8,128)(2,1)} %get-tuple-element.41), channel_id=1, source_target_pairs={{0,6},{1,25},{2,0},{3,27},{4,2},{5,29},{6,4},{7,31},{8,14},{9,1},{... | collective-permute-start | bytes 1572872 | tf_op jit(solution)/shard_map/ppermute | solution.py:323
  133.9 9.4 %collective-permute-start.3 = (bf16[2,64,2048]{2,1,0:T(8,128)(2,1)}, bf16[2,64,2048]{2,1,0:T(8,128)(2,1)S(1)}, u32[]{:S(2)}, u32[]{:S(2)}) collective-permute-start(bf16[2,64,2048]{2,1,0:T(8,128)(2,1)} %get-tuple-element.39), channel_id=1, source_target_pairs={{0,2},{1,9},{2,4},{3,11},{4,6},{5,13},{6,0},{7,15},{8,10},{9,17},{... | collective-permute-start | bytes 1572872 | tf_op jit(solution)/shard_map/ppermute | solution.py:344
  135.1 9.4 %collective-permute-start.6 = (bf16[2,64,2048]{2,1,0:T(8,128)(2,1)}, bf16[2,64,2048]{2,1,0:T(8,128)(2,1)S(1)}, u32[]{:S(2)}, u32[]{:S(2)}) collective-permute-start(bf16[2,64,2048]{2,1,0:T(8,128)(2,1)} %get-tuple-element.42), channel_id=1, source_target_pairs={{0,6},{1,25},{2,0},{3,27},{4,2},{5,29},{6,4},{7,31},{8,14},{9,1},{... | collective-permute-start | bytes 1572872 | tf_op jit(solution)/shard_map/ppermute | solution.py:345
  142.1 5.9 %copy-start.3 = (bf16[2,64,2048]{2,1,0:T(8,128)(2,1)}, bf16[2,64,2048]{2,1,0:T(8,128)(2,1)S(1)}, u32[]{:S(2)}) copy-start(bf16[2,64,2048]{2,1,0:T(8,128)(2,1)S(1)} %collective-permute-done.4.low_b_ref) | copy-start | bytes 1572868
  142.2 5.9 %copy-start.4 = (bf16[2,64,2048]{2,1,0:T(8,128)(2,1)}, bf16[2,64,2048]{2,1,0:T(8,128)(2,1)S(1)}, u32[]{:S(2)}) copy-start(bf16[2,64,2048]{2,1,0:T(8,128)(2,1)S(1)} %collective-permute-done.5.high_a_ref) | copy-start | bytes 1572868
  143.3 4.8 %copy-start.5 = (bf16[2,64,2048]{2,1,0:T(8,128)(2,1)}, bf16[2,64,2048]{2,1,0:T(8,128)(2,1)S(1)}, u32[]{:S(2)}) copy-start(bf16[2,64,2048]{2,1,0:T(8,128)(2,1)S(1)} %collective-permute-done.3.low_a_ref) | copy-start | bytes 1572868
  144.5 3.6 %copy-start.6 = (bf16[2,64,2048]{2,1,0:T(8,128)(2,1)}, bf16[2,64,2048]{2,1,0:T(8,128)(2,1)S(1)}, u32[]{:S(2)}) copy-start(bf16[2,64,2048]{2,1,0:T(8,128)(2,1)S(1)} %collective-permute-done.6.high_b_ref) | copy-start | bytes 1572868
  144.5 31.0 %all-to-all-start.3 = ((bf16[8,64,1024]{2,1,0:T(8,128)(2,1)}), bf16[8,64,1024]{2,1,0:T(8,128)(2,1)S(1)}, u32[]{:S(2)}, u32[]{:S(2)}) async-start(bf16[8,64,1024]{2,1,0:T(8,128)(2,1)} %add_rows.1), calls=%async_computation.3 | async-start | bytes 2097152 | tf_op jit(solution)/shard_map/all_to_all | solution.py:245
  151.7 7.8 %collective-permute-start.7 = (bf16[64,2048]{1,0:T(8,128)(2,1)}, bf16[64,2048]{1,0:T(8,128)(2,1)S(1)}, u32[]{:S(2)}, u32[]{:S(2)}) collective-permute-start(bf16[64,2048]{1,0:T(8,128)(2,1)} %get-tuple-element.49), channel_id=1, source_target_pairs={{0,8},{1,3},{2,10},{3,5},{4,12},{5,7},{6,14},{7,1},{8,16},{9,11},{... | collective-permute-start | bytes 786440 | tf_op jit(solution)/shard_map/ppermute | solution.py:362
  153.2 10.3 %collective-permute-start.8 = (bf16[64,2048]{1,0:T(8,128)(2,1)}, bf16[64,2048]{1,0:T(8,128)(2,1)S(1)}, u32[]{:S(2)}, u32[]{:S(2)}) collective-permute-start(bf16[64,2048]{1,0:T(8,128)(2,1)} %get-tuple-element.50), channel_id=1, source_target_pairs={{0,16},{1,5},{2,18},{3,7},{4,20},{5,1},{6,22},{7,3},{8,24},{9,13},... | collective-permute-start | bytes 786440 | tf_op jit(solution)/shard_map/ppermute | solution.py:362
  156.1 7.4 %collective-permute-start.9 = (bf16[64,2048]{1,0:T(8,128)(2,1)}, bf16[64,2048]{1,0:T(8,128)(2,1)S(1)}, u32[]{:S(2)}, u32[]{:S(2)}) collective-permute-start(bf16[64,2048]{1,0:T(8,128)(2,1)} %get-tuple-element.51), channel_id=1, source_target_pairs={{0,24},{1,7},{2,26},{3,1},{4,28},{5,3},{6,30},{7,5},{8,0},{9,15},{... | collective-permute-start | bytes 786440 | tf_op jit(solution)/shard_map/ppermute | solution.py:362
  164.6 1.4 collective-permute-start.10
  191.0 15.5 %all-to-all-start.5 = ((bf16[8,8,2048]{2,1,0:T(8,128)(2,1)}), bf16[8,8,2048]{2,1,0:T(8,128)(2,1)S(1)}, u32[]{:S(2)}, u32[]{:S(2)}) async-start(bf16[8,8,2048]{2,1,0:T(8,128)(2,1)} %broadcast_in_dim.15), calls=%async_computation.5 | async-start | bytes 524288 | tf_op jit(solution)/shard_map/all_to_all | solution.py:245
  (3 other events, 4.4 us)
Sparse Core Ops, SparseCore 0:
  10.6 60.8 all-gather.1

commit v5 on v4

--- a/solution.py
+++ b/solution.py
@@ -321,11 +321,13 @@
     down = lax.ppermute(far_b, "nbr", minus)
     low_b = lax.ppermute(ahead_b, "nbr", plus)
     high_a = lax.ppermute(behind_a, "nbr", minus)
+    add_spec = pl.BlockSpec((1, *up.shape[1:]), lambda i: (i, 0, 0))
     ahead_a, behind_b = pl.pallas_call(
         add_kernel,
+        grid=(2,),
         out_shape=[jax.ShapeDtypeStruct(up.shape, BF16)] * 2,
-        in_specs=[vmem] * 4,
-        out_specs=[vmem] * 2,
+        in_specs=[add_spec] * 4,
+        out_specs=[add_spec] * 2,
         compiler_params=pltpu.CompilerParams(vmem_limit_bytes=58 << 20),
         cost_estimate=pl.CostEstimate(flops=0, bytes_accessed=1 << 10, transcendentals=0),
         name="add_two",

time: 215 us -> 215 us (level)
  no operation moved by 1% of the time
where the time goes in v5:
time: 215 us; the launch traced here: 214 us
  waiting for transfers between devices  72.4 us (34%)
  blocking collectives  54.5 us (25%)
  Pallas kernels  39.5 us (18%)
  starting transfers between devices  26.3 us (12%)
  between operations  14.3 us (7%)
  local copies, waits for them, and re-layouts  4.56 us (2%)
  other arithmetic  2.42 us (1%)
    all_to_all x2, blocking collectives, swap(): return lax.all_to_all(array, 'seq', split_axis=0, concat_axis=0, tiled=True)  54.5 us
    all_to_all x4, waiting for transfers between devices, swap(): return lax.all_to_all(array, 'seq', split_axis=0, concat_axis=0, tiled=True)  51.6 us
    pallas_call x1, Pallas kernels, attend_call(): pl.pallas_call(functools.partial(main_kernel, spans=spans, span_length=sp...  24.7 us
    all_to_all x4, starting transfers between devices, swap(): return lax.all_to_all(array, 'seq', split_axis=0, concat_axis=0, tiled=True)  14.1 us
    ppermute x3, waiting for transfers between devices, body(): part = part + lax.ppermute(other, 'nbr', shifted(1, d + 1)).astype(F32)  6.02 us
    ppermute x3, starting transfers between devices, body(): part = part + lax.ppermute(other, 'nbr', shifted(1, d + 1)).astype(F32)  5.83 us
    ppermute x1, waiting for transfers between devices, body(): up = lax.ppermute(far_a, 'nbr', plus)  5.34 us
    pallas_call x1, Pallas kernels, pair_call(): pl.pallas_call(pair_kernel, grid=(cols // width,), out_shape=[block_shape...  5.2 us
  transfers between devices with their start and end apart: 16, of which 12 were waited for; matrix products, arithmetic and copies ran while one was open for 2% of the time, Pallas kernels for 7%

profile of v5, /device:TPU:2, one launch (start us, length us, event | category | flops | bytes accessed | tf_op | source)
XLA Modules:
  0.0 214.0 jit_solution(15707360846457724681)
XLA Ops:
  9.5 39.8 %all_to_all.30.stored_ref = bf16[8,72,1024]{2,1,0:T(8,128)(2,1)S(1)} all-to-all(bf16[8,72,1024]{2,1,0:T(8,128)(2,1)S(1)} %pad_maximum_fusion), channel_id=1, replica_groups=mesh['seq'=8,'nbr'=32] {'seq'}, dimensions={0} | all-to-all | bytes 2359296 | tf_op jit(solution)/shard_map/all_to_all | solution.py:245
  49.4 1.6 pick.1
  51.0 3.6 %all-to-all-start.1 = ((bf16[8,64,1024]{2,1,0:T(8,128)(2,1)}), bf16[8,64,1024]{2,1,0:T(8,128)(2,1)S(1)}, u32[]{:S(2)}, u32[]{:S(2)}) async-start(bf16[8,64,1024]{2,1,0:T(8,128)(2,1)} %pick.1), calls=%async_computation.1 | async-start | bytes 2097152 | tf_op jit(solution)/shard_map/all_to_all | solution.py:245
  54.6 27.5 %all-to-all-done.1 = bf16[8,64,1024]{2,1,0:T(8,128)(2,1)S(1)} async-done(((bf16[8,64,1024]{2,1,0:T(8,128)(2,1)}), bf16[8,64,1024]{2,1,0:T(8,128)(2,1)S(1)}, u32[]{:S(2)}, u32[]{:S(2)}) %all-to-all-start.1) | async-done | bytes 1048608 | tf_op jit(solution)/shard_map/all_to_all | solution.py:245
  82.1 24.7 %attend.1 = (bf16[128,2048]{1,0:T(8,128)(2,1)}, bf16[128,2048]{1,0:T(8,128)(2,1)}, bf16[4,4,64,2048]{3,2,1,0:T(8,128)(2,1)}, bf16[4,4,64,2048]{3,2,1,0:T(8,128)(2,1)}, bf16[8,2,32,1024]{3,2,1,0:T(8,128)(2,1)}) custom-call(s32[1]{0:T(128)} %bitcast.refs_0_, bf16[8,2,32,1024]{3,2,1,0:T(8,128)(2,1)S(1)} %bitcast.30, f32[1,1024]{1,0:T(1,128)S(1)} %bitcast.31, ...), custom_call_target="tpu_custom_call" | custom-call | flops 14000000000 | bytes 25165824 | tf_op jit(solution)/shard_map/attend/pallas_call | solution.py:203
  106.9 3.6 %all-to-all-start.2 = ((bf16[8,64,1024]{2,1,0:T(8,128)(2,1)}), bf16[8,64,1024]{2,1,0:T(8,128)(2,1)S(1)}, u32[]{:S(2)}, u32[]{:S(2)}) async-start(bf16[8,64,1024]{2,1,0:T(8,128)(2,1)} %bitcast.9), calls=%async_computation.2 | async-start | bytes 2097152 | tf_op jit(solution)/shard_map/all_to_all | solution.py:245
  110.6 3.8 %collective-permute-done.got_ref = bf16[4,4,64,2048]{3,2,1,0:T(8,128)(2,1)} collective-permute-done((bf16[4,4,64,2048]{3,2,1,0:T(8,128)(2,1)}, bf16[4,4,64,2048]{3,2,1,0:T(8,128)(2,1)}, u32[]{:S(2)}, u32[]{:S(2)}) %collective-permute-start) | collective-permute-done | bytes 4194336 | tf_op jit(solution)/shard_map/ppermute | solution.py:316
  114.4 5.2 %pair_add.1 = (bf16[4,64,2048]{2,1,0:T(8,128)(2,1)}, bf16[2,64,2048]{2,1,0:T(8,128)(2,1)}, bf16[2,64,2048]{2,1,0:T(8,128)(2,1)}, bf16[2,64,2048]{2,1,0:T(8,128)(...) custom-call(s32[1]{0:T(128)} %bitcast.8.at_ref, ...), custom_call_target="tpu_custom_call" | custom-call | bytes 1024 | tf_op jit(solution)/shard_map/pair_add/pallas_call | solution.py:64
  119.6 1.5 collective-permute-start.1
  121.6 1.5 collective-permute-start.4
  123.7 5.3 %collective-permute-done.1.b_ref = bf16[2,64,2048]{2,1,0:T(8,128)(2,1)S(1)} collective-permute-done((bf16[2,64,2048]{2,1,0:T(8,128)(2,1)}, bf16[2,64,2048]{2,1,0:T(8,128)(2,1)S(1)}, u32[]{:S(2)}, u32[]{:S(2)}) %collective-permute-start.1) | collective-permute-done | bytes 524320 | tf_op jit(solution)/shard_map/ppermute | solution.py:320
  131.3 2.4 %add_two.1 = (bf16[2,64,2048]{2,1,0:T(8,128)(2,1)}, bf16[2,64,2048]{2,1,0:T(8,128)(2,1)}) custom-call(bf16[2,64,2048]{2,1,0:T(8,128)(2,1)} %get-tuple-element.35.a_ref, bf16[2,64,2048]{2,1,0:T(8,128)(2,1)} %copy-done.7, bf16[2,64,2048]{2,1,0:T(8,128)(2,1)} %get-tuple-element.37.c_ref, bf16[2,64,2048]{2,1,0:T(8,128)(2,1)} %copy-done.8), custom_call_target="tpu_custom_call" | custom-call | bytes 1024 | tf_op jit(solution)/shard_map/add_two/pallas_call | solution.py:325
  135.7 4.4 %all-to-all-done.2.grads_ref = bf16[8,64,1024]{2,1,0:T(8,128)(2,1)S(1)} async-done(((bf16[8,64,1024]{2,1,0:T(8,128)(2,1)}), bf16[8,64,1024]{2,1,0:T(8,128)(2,1)S(1)}, u32[]{:S(2)}, u32[]{:S(2)}) %all-to-all-start.2) | async-done | bytes 1048608 | tf_op jit(solution)/shard_map/all_to_all | solution.py:245
  140.1 2.0 add_rows.1
  144.2 3.6 %all-to-all-start.3 = ((bf16[8,64,1024]{2,1,0:T(8,128)(2,1)}), bf16[8,64,1024]{2,1,0:T(8,128)(2,1)S(1)}, u32[]{:S(2)}, u32[]{:S(2)}) async-start(bf16[8,64,1024]{2,1,0:T(8,128)(2,1)} %add_rows.1), calls=%async_computation.3 | async-start | bytes 2097152 | tf_op jit(solution)/shard_map/all_to_all | solution.py:245
  147.8 3.6 %ring_add.1 = (bf16[64,2048]{1,0:T(8,128)(2,1)}, bf16[64,2048]{1,0:T(8,128)(2,1)}, bf16[64,2048]{1,0:T(8,128)(2,1)}, bf16[64,2048]{1,0:T(8,128)(2,1)}) custom-call(s32[1]{0:T(128)} %bitcast.7.at_ref, bf16[4,64,2048]{2,1,0:T(8,128)(2,1)} %get-tuple-element.34.stay_ref, bf16[2,64,2048]{2,1,0:T(8,128)(2,1)} %copy-done.5, bf16[2,64,2048]{2,1,0:T(8,128)(2,1)} %copy-done.3, ...), custom_call_target="tpu_custom_call" | custom-call | bytes 1024 | tf_op jit(solution)/shard_map/ring_add/pallas_call | solution.py:352
  151.4 1.6 collective-permute-start.7
  153.0 2.9 %collective-permute-start.8 = (bf16[64,2048]{1,0:T(8,128)(2,1)}, bf16[64,2048]{1,0:T(8,128)(2,1)S(1)}, u32[]{:S(2)}, u32[]{:S(2)}) collective-permute-start(bf16[64,2048]{1,0:T(8,128)(2,1)} %get-tuple-element.50), channel_id=1, source_target_pairs={{0,16},{1,5},{2,18},{3,7},{4,20},{5,1},{6,22},{7,3},{8,24},{9,13},... | collective-permute-start | bytes 786440 | tf_op jit(solution)/shard_map/ppermute | solution.py:364
  157.3 2.0 collective-permute-done.7
  159.2 4.0 %collective-permute-done.8 = bf16[64,2048]{1,0:T(8,128)(2,1)S(1)} collective-permute-done((bf16[64,2048]{1,0:T(8,128)(2,1)}, bf16[64,2048]{1,0:T(8,128)(2,1)S(1)}, u32[]{:S(2)}, u32[]{:S(2)}) %collective-permute-start.8) | collective-permute-done | bytes 262176 | tf_op jit(solution)/shard_map/ppermute | solution.py:364
  165.8 9.4 %all-to-all-done.3 = bf16[8,64,1024]{2,1,0:T(8,128)(2,1)S(1)} async-done(((bf16[8,64,1024]{2,1,0:T(8,128)(2,1)}), bf16[8,64,1024]{2,1,0:T(8,128)(2,1)S(1)}, u32[]{:S(2)}, u32[]{:S(2)}) %all-to-all-start.3) | async-done | bytes 1048608 | tf_op jit(solution)/shard_map/all_to_all | solution.py:245
  175.3 14.7 %all_to_all.31 = bf16[8,8,2048]{2,1,0:T(8,128)(2,1)S(1)} all-to-all(bf16[8,8,2048]{2,1,0:T(8,128)(2,1)S(1)} %pad_maximum_fusion.2), channel_id=1, replica_groups=mesh['seq'=8,'nbr'=32] {'seq'}, dimensions={0} | all-to-all | bytes 524288 | tf_op jit(solution)/shard_map/all_to_all | solution.py:245
  190.8 3.4 %all-to-all-start.5 = ((bf16[8,8,2048]{2,1,0:T(8,128)(2,1)}), bf16[8,8,2048]{2,1,0:T(8,128)(2,1)S(1)}, u32[]{:S(2)}, u32[]{:S(2)}) async-start(bf16[8,8,2048]{2,1,0:T(8,128)(2,1)} %broadcast_in_dim.15), calls=%async_computation.5 | async-start | bytes 524288 | tf_op jit(solution)/shard_map/all_to_all | solution.py:245
  195.9 10.4 %all-to-all-done.5 = bf16[8,8,2048]{2,1,0:T(8,128)(2,1)S(1)} async-done(((bf16[8,8,2048]{2,1,0:T(8,128)(2,1)}), bf16[8,8,2048]{2,1,0:T(8,128)(2,1)S(1)}, u32[]{:S(2)}, u32[]{:S(2)}) %all-to-all-start.5) | async-done | bytes 262176 | tf_op jit(solution)/shard_map/all_to_all | solution.py:245
  (58 shorter events, 17.3 us)
Async XLA Ops:
  7.2 2.1 copy-start.10
  7.2 74.9 %all-gather.2.cloned.1.call-start = ((), (), s32[]{:S(2)}) async-start(), calls=%async_computation.6 | async-start | bytes 8650752 | tf_op jit(solution)/shard_map/all_gather | solution.py:262
  49.4 32.7 %copy-start = (bf16[128,2048]{1,0:T(8,128)(2,1)S(1)}, bf16[128,2048]{1,0:T(8,128)(2,1)}, u32[]{:S(2)}) copy-start(bf16[128,2048]{1,0:T(8,128)(2,1)} %refs_5_.1) | copy-start | bytes 1572868
  49.4 32.7 %copy-start.1 = (bf16[128,2048]{1,0:T(8,128)(2,1)S(1)}, bf16[128,2048]{1,0:T(8,128)(2,1)}, u32[]{:S(2)}) copy-start(bf16[128,2048]{1,0:T(8,128)(2,1)} %refs_6_.1) | copy-start | bytes 1572868
  49.4 32.7 %copy-start.2 = (f32[1024]{0:T(1024)S(1)}, f32[1024]{0:T(1024)}, u32[]{:S(2)}) copy-start(f32[1024]{0:T(1024)} %param.12) | copy-start | bytes 12292
  51.0 31.1 %all-to-all-start.1 = ((bf16[8,64,1024]{2,1,0:T(8,128)(2,1)}), bf16[8,64,1024]{2,1,0:T(8,128)(2,1)S(1)}, u32[]{:S(2)}, u32[]{:S(2)}) async-start(bf16[8,64,1024]{2,1,0:T(8,128)(2,1)} %pick.1), calls=%async_computation.1 | async-start | bytes 2097152 | tf_op jit(solution)/shard_map/all_to_all | solution.py:245
  106.8 7.6 %collective-permute-start = (bf16[4,4,64,2048]{3,2,1,0:T(8,128)(2,1)}, bf16[4,4,64,2048]{3,2,1,0:T(8,128)(2,1)}, u32[]{:S(2)}, u32[]{:S(2)}) collective-permute-start(bf16[4,4,64,2048]{3,2,1,0:T(8,128)(2,1)} %get-tuple-element.33), channel_id=1, source_target_pairs={{0,1},{1,0},{2,3},{3,2},{4,5},{5,4},{6,7},{7,6},{8,9},{9,8},{10,11... | collective-permute-start | bytes 12582920 | tf_op jit(solution)/shard_map/ppermute | solution.py:316
  106.9 33.2 %all-to-all-start.2 = ((bf16[8,64,1024]{2,1,0:T(8,128)(2,1)}), bf16[8,64,1024]{2,1,0:T(8,128)(2,1)S(1)}, u32[]{:S(2)}, u32[]{:S(2)}) async-start(bf16[8,64,1024]{2,1,0:T(8,128)(2,1)} %bitcast.9), calls=%async_computation.2 | async-start | bytes 2097152 | tf_op jit(solution)/shard_map/all_to_all | solution.py:245
  119.6 9.4 %collective-permute-start.1 = (bf16[2,64,2048]{2,1,0:T(8,128)(2,1)}, bf16[2,64,2048]{2,1,0:T(8,128)(2,1)S(1)}, u32[]{:S(2)}, u32[]{:S(2)}) collective-permute-start(bf16[2,64,2048]{2,1,0:T(8,128)(2,1)} %get-tuple-element.36), channel_id=1, source_target_pairs={{0,2},{1,9},{2,4},{3,11},{4,6},{5,13},{6,0},{7,15},{8,10},{9,17},{... | collective-permute-start | bytes 1572872 | tf_op jit(solution)/shard_map/ppermute | solution.py:320
  121.1 9.4 %collective-permute-start.2 = (bf16[2,64,2048]{2,1,0:T(8,128)(2,1)}, bf16[2,64,2048]{2,1,0:T(8,128)(2,1)S(1)}, u32[]{:S(2)}, u32[]{:S(2)}) collective-permute-start(bf16[2,64,2048]{2,1,0:T(8,128)(2,1)} %get-tuple-element.38), channel_id=1, source_target_pairs={{0,6},{1,25},{2,0},{3,27},{4,2},{5,29},{6,4},{7,31},{8,14},{9,1},{... | collective-permute-start | bytes 1572872 | tf_op jit(solution)/shard_map/ppermute | solution.py:321
  121.6 20.5 %collective-permute-start.4 = (bf16[2,64,2048]{2,1,0:T(8,128)(2,1)}, bf16[2,64,2048]{2,1,0:T(8,128)(2,1)S(1)}, u32[]{:S(2)}, u32[]{:S(2)}) collective-permute-start(bf16[2,64,2048]{2,1,0:T(8,128)(2,1)} %get-tuple-element.40), channel_id=1, source_target_pairs={{0,2},{1,9},{2,4},{3,11},{4,6},{5,13},{6,0},{7,15},{8,10},{9,17},{... | collective-permute-start | bytes 1572872 | tf_op jit(solution)/shard_map/ppermute | solution.py:322
  123.1 19.0 %collective-permute-start.5 = (bf16[2,64,2048]{2,1,0:T(8,128)(2,1)}, bf16[2,64,2048]{2,1,0:T(8,128)(2,1)S(1)}, u32[]{:S(2)}, u32[]{:S(2)}) collective-permute-start(bf16[2,64,2048]{2,1,0:T(8,128)(2,1)} %get-tuple-element.41), channel_id=1, source_target_pairs={{0,6},{1,25},{2,0},{3,27},{4,2},{5,29},{6,4},{7,31},{8,14},{9,1},{... | collective-permute-start | bytes 1572872 | tf_op jit(solution)/shard_map/ppermute | solution.py:323
  133.6 9.4 %collective-permute-start.3 = (bf16[2,64,2048]{2,1,0:T(8,128)(2,1)}, bf16[2,64,2048]{2,1,0:T(8,128)(2,1)S(1)}, u32[]{:S(2)}, u32[]{:S(2)}) collective-permute-start(bf16[2,64,2048]{2,1,0:T(8,128)(2,1)} %get-tuple-element.39), channel_id=1, source_target_pairs={{0,2},{1,9},{2,4},{3,11},{4,6},{5,13},{6,0},{7,15},{8,10},{9,17},{... | collective-permute-start | bytes 1572872 | tf_op jit(solution)/shard_map/ppermute | solution.py:346
  134.8 9.4 %collective-permute-start.6 = (bf16[2,64,2048]{2,1,0:T(8,128)(2,1)}, bf16[2,64,2048]{2,1,0:T(8,128)(2,1)S(1)}, u32[]{:S(2)}, u32[]{:S(2)}) collective-permute-start(bf16[2,64,2048]{2,1,0:T(8,128)(2,1)} %get-tuple-element.42), channel_id=1, source_target_pairs={{0,6},{1,25},{2,0},{3,27},{4,2},{5,29},{6,4},{7,31},{8,14},{9,1},{... | collective-permute-start | bytes 1572872 | tf_op jit(solution)/shard_map/ppermute | solution.py:347
  142.1 5.7 %copy-start.3 = (bf16[2,64,2048]{2,1,0:T(8,128)(2,1)}, bf16[2,64,2048]{2,1,0:T(8,128)(2,1)S(1)}, u32[]{:S(2)}) copy-start(bf16[2,64,2048]{2,1,0:T(8,128)(2,1)S(1)} %collective-permute-done.4.low_b_ref) | copy-start | bytes 1572868
  142.2 5.7 %copy-start.4 = (bf16[2,64,2048]{2,1,0:T(8,128)(2,1)}, bf16[2,64,2048]{2,1,0:T(8,128)(2,1)S(1)}, u32[]{:S(2)}) copy-start(bf16[2,64,2048]{2,1,0:T(8,128)(2,1)S(1)} %collective-permute-done.5.high_a_ref) | copy-start | bytes 1572868
  143.0 4.8 %copy-start.5 = (bf16[2,64,2048]{2,1,0:T(8,128)(2,1)}, bf16[2,64,2048]{2,1,0:T(8,128)(2,1)S(1)}, u32[]{:S(2)}) copy-start(bf16[2,64,2048]{2,1,0:T(8,128)(2,1)S(1)} %collective-permute-done.3.low_a_ref) | copy-start | bytes 1572868
  144.2 3.6 %copy-start.6 = (bf16[2,64,2048]{2,1,0:T(8,128)(2,1)}, bf16[2,64,2048]{2,1,0:T(8,128)(2,1)S(1)}, u32[]{:S(2)}) copy-start(bf16[2,64,2048]{2,1,0:T(8,128)(2,1)S(1)} %collective-permute-done.6.high_b_ref) | copy-start | bytes 1572868
  144.2 31.0 %all-to-all-start.3 = ((bf16[8,64,1024]{2,1,0:T(8,128)(2,1)}), bf16[8,64,1024]{2,1,0:T(8,128)(2,1)S(1)}, u32[]{:S(2)}, u32[]{:S(2)}) async-start(bf16[8,64,1024]{2,1,0:T(8,128)(2,1)} %add_rows.1), calls=%async_computation.3 | async-start | bytes 2097152 | tf_op jit(solution)/shard_map/all_to_all | solution.py:245
  151.4 7.8 %collective-permute-start.7 = (bf16[64,2048]{1,0:T(8,128)(2,1)}, bf16[64,2048]{1,0:T(8,128)(2,1)S(1)}, u32[]{:S(2)}, u32[]{:S(2)}) collective-permute-start(bf16[64,2048]{1,0:T(8,128)(2,1)} %get-tuple-element.49), channel_id=1, source_target_pairs={{0,8},{1,3},{2,10},{3,5},{4,12},{5,7},{6,14},{7,1},{8,16},{9,11},{... | collective-permute-start | bytes 786440 | tf_op jit(solution)/shard_map/ppermute | solution.py:364
  153.0 10.3 %collective-permute-start.8 = (bf16[64,2048]{1,0:T(8,128)(2,1)}, bf16[64,2048]{1,0:T(8,128)(2,1)S(1)}, u32[]{:S(2)}, u32[]{:S(2)}) collective-permute-start(bf16[64,2048]{1,0:T(8,128)(2,1)} %get-tuple-element.50), channel_id=1, source_target_pairs={{0,16},{1,5},{2,18},{3,7},{4,20},{5,1},{6,22},{7,3},{8,24},{9,13},... | collective-permute-start | bytes 786440 | tf_op jit(solution)/shard_map/ppermute | solution.py:364
  155.9 7.4 %collective-permute-start.9 = (bf16[64,2048]{1,0:T(8,128)(2,1)}, bf16[64,2048]{1,0:T(8,128)(2,1)S(1)}, u32[]{:S(2)}, u32[]{:S(2)}) collective-permute-start(bf16[64,2048]{1,0:T(8,128)(2,1)} %get-tuple-element.51), channel_id=1, source_target_pairs={{0,24},{1,7},{2,26},{3,1},{4,28},{5,3},{6,30},{7,5},{8,0},{9,15},{... | collective-permute-start | bytes 786440 | tf_op jit(solution)/shard_map/ppermute | solution.py:364
  164.4 1.4 collective-permute-start.10
  190.8 15.5 %all-to-all-start.5 = ((bf16[8,8,2048]{2,1,0:T(8,128)(2,1)}), bf16[8,8,2048]{2,1,0:T(8,128)(2,1)S(1)}, u32[]{:S(2)}, u32[]{:S(2)}) async-start(bf16[8,8,2048]{2,1,0:T(8,128)(2,1)} %broadcast_in_dim.15), calls=%async_computation.5 | async-start | bytes 524288 | tf_op jit(solution)/shard_map/all_to_all | solution.py:245
  (3 other events, 4.4 us)
Sparse Core Ops, SparseCore 0:
  10.6 60.8 all-gather.1
